TPU v7x, 256 devices: a whole 4x4x8 slice. The times are simulated.
256 devices in a mesh: pts: 32 (over x, z_hi, core), ctr: 8 (over z_lo, y).
Axes of the slice: x: 4, y: 4, z: 8 (z_hi: 4, z_lo: 2; z = z_hi * 2 + z_lo), core: 2. Of those that a mesh axis runs over, the one named last changes fastest.
Arguments:
- embeddings: bfloat16 [16384, 128], P('pts'), may hold values from -1.1953125 to 1.1953125
- centres: bfloat16 [65536, 128], P('ctr'), may hold values from -1.1953125 to 1.1953125
- prior_freq: float32 [65536], P('ctr'), may hold values from 0.1 to 1
Outputs:
- embed_grad: float32 [16384, 128], P('pts')
- centre_grad: float32 [8, 8192, 128], P('ctr', 'pts')
All inputs are finite; a program needn't handle non-finite values.
Results may differ from a plain program's by a relative error of at most 0.0003.
Values sent between devices are 32-bit elements; how exact they have to be, the bound alone decides.
No kernel may reach another device: no remote copies, remote signals or barrier semaphores. Data moves between devices by JAX's collectives and lax.ppermute only.
A program may use at most 64 MiB of HBM per device.

v0:
```python
import math

import jax
import jax.numpy as jnp
from jax import lax
from jax.sharding import PartitionSpec as P

loss_scale = 64.0


def kernel(points, point_norms, block):
    cross = jnp.dot(points, block.T, preferred_element_type=jnp.float32)
    block_norms = jnp.sum(jnp.square(block.astype(jnp.float32)), axis=1)
    dist = point_norms[:, None] + block_norms[None, :] - 2.0 * cross
    return 1.0 / (1.0 + dist)


def body(embeddings, centres, prior_freq):
    points_wide = embeddings.astype(jnp.float32)
    point_norms = jnp.sum(points_wide * points_wide, axis=1)
    width = centres.shape[1]
    local_count = centres.shape[0]
    block_size = math.gcd(local_count, 1024)
    block_count = local_count // block_size
    blocks = centres.reshape(block_count, block_size, width)
    priors = prior_freq.reshape(block_count, block_size)

    def row_part(block):
        return jnp.sum(kernel(embeddings, point_norms, block), axis=1)

    row_total = lax.psum(jnp.sum(lax.map(row_part, blocks), axis=0), "ctr")

    def freq_part(block):
        return jnp.sum(kernel(embeddings, point_norms, block) / row_total[:, None], axis=0)

    freqs = lax.psum(lax.map(freq_part, blocks), "pts") + priors
    empty = jnp.zeros(points_wide.shape, jnp.float32)

    def target_part(pair):
        block, freq = pair
        kern = kernel(embeddings, point_norms, block)
        return jnp.sum(kern * kern / freq[None, :], axis=1)

    target_total = lax.psum(jnp.sum(lax.map(target_part, (blocks, freqs)), axis=0), "ctr")

    def embed_step(carry, pair):
        block, freq = pair
        kern = kernel(embeddings, point_norms, block)
        block_wide = block.astype(jnp.float32)
        weight = kern * (
            kern * kern / (freq[None, :] * target_total[:, None]) - kern / row_total[:, None]
        )
        return (
            carry
            + jnp.sum(weight, axis=1)[:, None] * points_wide
            - jnp.dot(weight, block_wide, precision=lax.Precision.HIGHEST),
            None,
        )

    embed_part, unused = lax.scan(embed_step, empty, (blocks, freqs))
    embed_grad = 2.0 * loss_scale * lax.psum(embed_part, "ctr")
    freq_flat = freqs.reshape(local_count)
    rows = local_count // lax.axis_size("pts")
    inner = math.gcd(rows * lax.axis_size("pts"), 1024)
    pieces = rows * lax.axis_size("pts") // inner
    sub_blocks = centres.reshape(pieces, inner, width)
    sub_freqs = freq_flat.reshape(pieces, inner)

    def centre_block(pair):
        block, freq = pair
        kern = kernel(embeddings, point_norms, block)
        block_wide = block.astype(jnp.float32)
        weight = kern * (
            kern * kern / (freq[None, :] * target_total[:, None]) - kern / row_total[:, None]
        )
        return jnp.sum(weight, axis=0)[:, None] * block_wide - jnp.dot(
            weight.T, points_wide, precision=lax.Precision.HIGHEST
        )

    mine = lax.psum_scatter(
        lax.map(centre_block, (sub_blocks, sub_freqs)).reshape(rows * lax.axis_size("pts"), width),
        "pts",
        scatter_dimension=0,
        tiled=True,
    )
    centre_grad = (2.0 * loss_scale * mine).reshape(1, rows, width)
    return (embed_grad, centre_grad)


def solution(mesh):
    in_specs = (P("pts", None), P("ctr", None), P("ctr"))
    out_specs = (P("pts", None), P("ctr", "pts", None))
    return jax.shard_map(body, mesh=mesh, in_specs=in_specs, out_specs=out_specs, check_vma=False)
```

profile of v0, /device:TPU:32, one launch (start us, length us, event | category | flops | bytes accessed | tf_op | source)
XLA Modules:
  0.0 478.9 jit_solution(9765613112511529593)
XLA Ops:
  10.1 22.6 %while.51 = (s32[]{:T(128)}, f32[8,512]{1,0:T(8,128)S(1)}, f32[512]{0:T(512)S(1)}, bf16[8,1024,128]{2,1,0:T(8,128)(2,1)}, bf16[512,128]{1,0:T(8,128)(2,1)}, /*index=5*/s32[]{:T(128)}, s32[]{:T(128)}) while((s32[]{:T(128)}, f32[8,512]{1,0:T(8,128)S(1)}, f32[512]{0:T(512)S(1)}, bf16[8,1024,128]{2,1,0:T(8,128)(2,1)}, bf16[512,128]{1,0:T(8,128)(2,1)}, ...), condition=%wide.region_4.5_spmd, body=%wide.region_1.4_spmd.sunk | while | flops 137755136 | bytes 672341 | solution.py:31
  32.7 18.5 %psum.28 = f32[512]{0:T(512)S(1)} all-reduce(f32[512]{0:T(512)S(1)} %reduce_sum.118), channel_id=1, replica_groups=mesh['pts'=32,'ctr'=8] {'ctr'}, use_global_device_ids=true, to_apply=%region_6.7 | all-reduce | flops 512 | bytes 4096 | tf_op jit(solution)/shard_map/psum | solution.py:31
  51.2 23.6 %while.52 = (s32[]{:T(128)}, f32[8,1024]{1,0:T(8,128)S(1)}, f32[512]{0:T(512)S(1)}, bf16[8,1024,128]{2,1,0:T(8,128)(2,1)}, bf16[512,128]{1,0:T(8,128)(2,1)}, /*index=5*/f32[512]{0:T(512)S(1)}, s32[]{:T(128)}, s32[]{:T(128)}) while((s32[]{:T(128)}, f32[8,1024]{1,0:T(8,128)S(1)}, f32[512]{0:T(512)S(1)}, bf16[8,1024,128]{2,1,0:T(8,128)(2,1)}, ...), condition=%wide.region_10.11_spmd, body=%wide.region_7.10_spmd.sunk | while | flops 138278912 | bytes 680541 | solution.py:36
  74.8 142.3 %psum.29 = f32[8,1024]{1,0:T(8,128)S(1)} all-reduce(f32[8,1024]{1,0:T(8,128)S(1)} %get-tuple-element.188), channel_id=1, replica_groups=mesh['pts'=32,'ctr'=8] {'pts'}, use_global_device_ids=true, to_apply=%region_11.12 | all-reduce | flops 8192 | bytes 65536 | tf_op jit(solution)/shard_map/psum | solution.py:36
  217.1 24.0 %while.53 = (s32[]{:T(128)}, f32[8,512]{1,0:T(8,128)S(1)}, f32[512]{0:T(512)S(1)}, bf16[8,1024,128]{2,1,0:T(8,128)(2,1)}, bf16[512,128]{1,0:T(8,128)(2,1)}, /*index=5*/f32[8,1024]{1,0:T(8,128)S(1)}, s32[]{:T(128)}, s32[]{:T(128)}) while((s32[]{:T(128)}, f32[8,512]{1,0:T(8,128)S(1)}, f32[512]{0:T(512)S(1)}, ...), condition=%wide.region_15.16_spmd, body=%wide.region_12.15_spmd.sunk | while | flops 138803712 | bytes 684641 | solution.py:44
  241.2 16.0 %psum.30 = f32[512]{0:T(512)S(1)} all-reduce(f32[512]{0:T(512)S(1)} %reduce_sum.119), channel_id=1, replica_groups=mesh['pts'=32,'ctr'=8] {'ctr'}, use_global_device_ids=true, to_apply=%region_17.18 | all-reduce | flops 512 | bytes 4096 | tf_op jit(solution)/shard_map/psum | solution.py:44
  257.2 50.9 %while.55 = (s32[]{:T(128)}, f32[512,128]{1,0:T(8,128)S(1)}, f32[512]{0:T(512)S(1)}, bf16[8,1024,128]{2,1,0:T(8,128)(2,1)}, bf16[512,128]{1,0:T(8,128)(2,1)}, /*...) while((s32[]{:T(128)}, f32[512,128]{1,0:T(8,128)S(1)}, ...), condition=%wide.region_21.22_spmd.clone, body=%wide.region_18.21_spmd.clone.sunk | while | flops 946993664 | bytes 5930111 | solution.py:60
  267.1 2.8 convolution_subtract_fusion.3
  273.4 2.8 convolution_subtract_fusion.3
  279.8 2.8 convolution_subtract_fusion.3
  286.2 2.8 convolution_subtract_fusion.3
  292.5 2.8 convolution_subtract_fusion.3
  298.9 2.8 convolution_subtract_fusion.3
  305.3 2.8 convolution_subtract_fusion.3
  308.9 69.2 %while.54 = (s32[]{:T(128)}, f32[8,1024,128]{2,1,0:T(8,128)}, f32[512]{0:T(512)S(1)}, bf16[8,1024,128]{2,1,0:T(8,128)(2,1)}, bf16[512,128]{1,0:T(8,128)(2,1)}, /...) while((s32[]{:T(128)}, f32[8,1024,128]{2,1,0:T(8,128)}, ...), condition=%wide.region_26.27_spmd, body=%wide.region_23.26_spmd.sunk | while | flops 947124224 | bytes 5934189 | solution.py:81
  312.3 5.2 %fusion.78 = f32[8,1024,128]{2,1,0:T(8,128)} fusion(f32[8,1024,128]{2,1,0:T(8,128)} %get-tuple-element.632, s32[]{:T(128)} %get-tuple-element.631, f32[512,1024]{1,0:T(8,128)S(1)} %get-tuple-element.506, f32[512,128]{1,0:T(8,128)S(1)} %get-tuple-element.649, f32[1024]{0:T(1024)S(1)} %get-tuple-element.507, bf16[8,1024,128]{2,1,0:T(8,128)(2,1)} %get-tuple-element.644), kind=kOutput, calls=%fused_computation.33.clone.1 | convolution fusion | flops 805699584 | bytes 3150336 | tf_op jit(solution)/shard_map/while/body/eval_jaxpr/dot_general | solution.py:76
  320.9 5.2 %fusion.78 = f32[8,1024,128]{2,1,0:T(8,128)} fusion(f32[8,1024,128]{2,1,0:T(8,128)} %get-tuple-element.632, s32[]{:T(128)} %get-tuple-element.631, f32[512,1024]{1,0:T(8,128)S(1)} %get-tuple-element.506, f32[512,128]{1,0:T(8,128)S(1)} %get-tuple-element.649, f32[1024]{0:T(1024)S(1)} %get-tuple-element.507, bf16[8,1024,128]{2,1,0:T(8,128)(2,1)} %get-tuple-element.644), kind=kOutput, calls=%fused_computation.33.clone.1 | convolution fusion | flops 805699584 | bytes 3150336 | tf_op jit(solution)/shard_map/while/body/eval_jaxpr/dot_general | solution.py:76
  329.6 5.2 %fusion.78 = f32[8,1024,128]{2,1,0:T(8,128)} fusion(f32[8,1024,128]{2,1,0:T(8,128)} %get-tuple-element.632, s32[]{:T(128)} %get-tuple-element.631, f32[512,1024]{1,0:T(8,128)S(1)} %get-tuple-element.506, f32[512,128]{1,0:T(8,128)S(1)} %get-tuple-element.649, f32[1024]{0:T(1024)S(1)} %get-tuple-element.507, bf16[8,1024,128]{2,1,0:T(8,128)(2,1)} %get-tuple-element.644), kind=kOutput, calls=%fused_computation.33.clone.1 | convolution fusion | flops 805699584 | bytes 3150336 | tf_op jit(solution)/shard_map/while/body/eval_jaxpr/dot_general | solution.py:76
  338.2 5.2 %fusion.78 = f32[8,1024,128]{2,1,0:T(8,128)} fusion(f32[8,1024,128]{2,1,0:T(8,128)} %get-tuple-element.632, s32[]{:T(128)} %get-tuple-element.631, f32[512,1024]{1,0:T(8,128)S(1)} %get-tuple-element.506, f32[512,128]{1,0:T(8,128)S(1)} %get-tuple-element.649, f32[1024]{0:T(1024)S(1)} %get-tuple-element.507, bf16[8,1024,128]{2,1,0:T(8,128)(2,1)} %get-tuple-element.644), kind=kOutput, calls=%fused_computation.33.clone.1 | convolution fusion | flops 805699584 | bytes 3150336 | tf_op jit(solution)/shard_map/while/body/eval_jaxpr/dot_general | solution.py:76
  346.9 5.2 %fusion.78 = f32[8,1024,128]{2,1,0:T(8,128)} fusion(f32[8,1024,128]{2,1,0:T(8,128)} %get-tuple-element.632, s32[]{:T(128)} %get-tuple-element.631, f32[512,1024]{1,0:T(8,128)S(1)} %get-tuple-element.506, f32[512,128]{1,0:T(8,128)S(1)} %get-tuple-element.649, f32[1024]{0:T(1024)S(1)} %get-tuple-element.507, bf16[8,1024,128]{2,1,0:T(8,128)(2,1)} %get-tuple-element.644), kind=kOutput, calls=%fused_computation.33.clone.1 | convolution fusion | flops 805699584 | bytes 3150336 | tf_op jit(solution)/shard_map/while/body/eval_jaxpr/dot_general | solution.py:76
  355.5 5.2 %fusion.78 = f32[8,1024,128]{2,1,0:T(8,128)} fusion(f32[8,1024,128]{2,1,0:T(8,128)} %get-tuple-element.632, s32[]{:T(128)} %get-tuple-element.631, f32[512,1024]{1,0:T(8,128)S(1)} %get-tuple-element.506, f32[512,128]{1,0:T(8,128)S(1)} %get-tuple-element.649, f32[1024]{0:T(1024)S(1)} %get-tuple-element.507, bf16[8,1024,128]{2,1,0:T(8,128)(2,1)} %get-tuple-element.644), kind=kOutput, calls=%fused_computation.33.clone.1 | convolution fusion | flops 805699584 | bytes 3150336 | tf_op jit(solution)/shard_map/while/body/eval_jaxpr/dot_general | solution.py:76
  364.2 5.2 %fusion.78 = f32[8,1024,128]{2,1,0:T(8,128)} fusion(f32[8,1024,128]{2,1,0:T(8,128)} %get-tuple-element.632, s32[]{:T(128)} %get-tuple-element.631, f32[512,1024]{1,0:T(8,128)S(1)} %get-tuple-element.506, f32[512,128]{1,0:T(8,128)S(1)} %get-tuple-element.649, f32[1024]{0:T(1024)S(1)} %get-tuple-element.507, bf16[8,1024,128]{2,1,0:T(8,128)(2,1)} %get-tuple-element.644), kind=kOutput, calls=%fused_computation.33.clone.1 | convolution fusion | flops 805699584 | bytes 3150336 | tf_op jit(solution)/shard_map/while/body/eval_jaxpr/dot_general | solution.py:76
  372.8 5.2 %fusion.78 = f32[8,1024,128]{2,1,0:T(8,128)} fusion(f32[8,1024,128]{2,1,0:T(8,128)} %get-tuple-element.632, s32[]{:T(128)} %get-tuple-element.631, f32[512,1024]{1,0:T(8,128)S(1)} %get-tuple-element.506, f32[512,128]{1,0:T(8,128)S(1)} %get-tuple-element.649, f32[1024]{0:T(1024)S(1)} %get-tuple-element.507, bf16[8,1024,128]{2,1,0:T(8,128)(2,1)} %get-tuple-element.644), kind=kOutput, calls=%fused_computation.33.clone.1 | convolution fusion | flops 805699584 | bytes 3150336 | tf_op jit(solution)/shard_map/while/body/eval_jaxpr/dot_general | solution.py:76
  382.3 87.5 %reduce-scatter.2.cloned.1.call-done = f32[256,128]{1,0:T(8,128)} async-done(((f32[8192,128]{1,0:T(8,128)}), f32[256,128]{1,0:T(8,128)}) %reduce-scatter.2.cloned.1.call-update) | async-done | bytes 131088 | tf_op jit(solution)/shard_map/reduce_scatter | solution.py:80
  (151 shorter events, 135.9 us)
Async XLA Ops:
  8.0 372.7 %all-reduce.2.cloned.1.call-start = ((), (), s32[]{:S(2)}) async-start(), calls=%async_computation.1 | async-start | bytes 524288 | tf_op jit(solution)/shard_map/psum | solution.py:61
  51.2 165.9 %copy-start.1 = (f32[8192]{0:T(1024)S(1)}, f32[8192]{0:T(1024)}, u32[]{:S(2)}) copy-start(f32[8192]{0:T(1024)} %param.15) | copy-start | bytes 98308
  308.1 0.7 copy-start
  308.8 161.0 %reduce-scatter.2.cloned.1.call-start = ((), (), s32[]{:S(2)}) async-start(), calls=%async_computation.2 | async-start | bytes 4325376 | tf_op jit(solution)/shard_map/reduce_scatter | solution.py:80
Sparse Core Ops, SparseCore 0:
  308.9 71.6 all-reduce.1
Sparse Core Ops, SparseCore 1:
  378.1 91.7 reduce-scatter.1
where the time goes:
time: 483 us; the launch traced here: 479 us
  blocking collectives  177 us (37%)
  matrix products  140 us (29%)
  waiting for transfers between devices  90.2 us (19%)
  other arithmetic  51.7 us (11%)
  between operations  15.6 us (3%)
    psum x1, blocking collectives, body(): freqs = lax.psum(lax.map(freq_part, blocks), 'pts') + priors  142 us
    reduce_scatter x1, waiting for transfers between devices, body(): lax.psum_scatter(lax.map(centre_block, (sub_blocks, sub_freqs)).reshape(r...  87.5 us
    dot_general x40, matrix products, kernel(): cross = jnp.dot(points, block.T, preferred_element_type=jnp.float32)  75.9 us
    reduce_sum x40, other arithmetic, kernel(): block_norms = jnp.sum(jnp.square(block.astype(jnp.float32)), axis=1)  46.4 us
    dot_general x8, matrix products, centre_block(): jnp.dot(weight.T, points_wide, precision=lax.Precision.HIGHEST)  41.9 us
    dot_general x8, matrix products, embed_step(): jnp.dot(weight, block_wide, precision=lax.Precision.HIGHEST)  22.5 us
    psum x1, blocking collectives, body(): row_total = lax.psum(jnp.sum(lax.map(row_part, blocks), axis=0), 'ctr')  18.5 us
    psum x1, blocking collectives, body(): lax.psum(jnp.sum(lax.map(target_part, (blocks, freqs)), axis=0), 'ctr')  16 us
  transfers between devices with their start and end apart: 2, of which 2 were waited for; matrix products, arithmetic and copies ran while one was open for 15% of the time, Pallas kernels for 0%

commit v1 on v0

v1 whole, which is shorter than its diff:
```python
import jax
import jax.numpy as jnp
from jax import lax
from jax.experimental import pallas as pl
from jax.experimental.pallas import tpu as pltpu
from jax.sharding import PartitionSpec as P

SIDE = 4
CORES = 2
LANES = 128
ONES = 16
SCALE = 128.0
ROWS_X = 88
MIB = 2**20
F32 = jnp.float32
BF16 = jnp.bfloat16


def core_perm(size):
    return [(i, i ^ 1) for i in range(size)]


def x_perm(size, s):
    return [(i, i ^ (s * SIDE * CORES)) for i in range(size)]


def h_perm(size, s):
    return [(i, i ^ (s * CORES)) for i in range(size)]


def ctr_perm(size, s):
    return [(i, i ^ s) for i in range(size)]


def tile_lanes(column, width):
    return jnp.concatenate([column] * (width // LANES), axis=1)


def spread(row):
    return jnp.broadcast_to(row, (LANES, row.shape[1])).T


def four(refs):
    a, b, c, d = refs
    return (a[...] + b[...]) + (c[...] + d[...])


def kern_body(z_ref, zo_ref, c_ref, kern_ref, row_ref, ct_ref, zt_ref, za, zn, acc):
    half = z_ref.shape[0]
    step = 512
    for base, part in ((0, z_ref[...].astype(F32)), (half, zo_ref[...])):
        zn[base : base + half] = jnp.broadcast_to(
            jnp.sum(part * part, axis=1, keepdims=True) + 1.0, (half, LANES)
        )
        za[base : base + half] = (-2.0 * part).astype(BF16)
        zt_ref[:LANES, base : base + half] = (-SCALE * part.T).astype(BF16)
    zt_ref[LANES:] = jnp.full((ONES, 2 * half), SCALE, BF16)
    acc[...] = jnp.zeros_like(acc)

    @pl.loop(0, c_ref.shape[0] // step)
    def _(t):
        at = pl.ds(pl.multiple_of(t * step, step), step)
        ct = c_ref[at, :].astype(F32).T
        ct_ref[:, at] = ct
        norms = jnp.sum(ct * ct, axis=0, keepdims=True)
        cross = jnp.dot(za[...], ct.astype(BF16), preferred_element_type=F32)
        kern = 1.0 / (cross + norms + tile_lanes(zn[...], step))
        kern_ref[:, at] = kern
        total = acc[...]
        for g in range(step // LANES):
            total = total + kern[:, g * LANES : (g + 1) * LANES]
        acc[...] = total

    row_ref[...] = jnp.sum(acc[...].T, axis=0, keepdims=True)


def freq_body(kern_ref, r0, r1, r2, r3, f_ref, rinv_ref):
    points, count = kern_ref.shape
    rinv = 1.0 / four((r0, r1, r2, r3))
    rinv_ref[...] = rinv
    spread_r = spread(rinv)
    for g in range(count // LANES):
        at = slice(g * LANES, (g + 1) * LANES)
        total = jnp.zeros((8, LANES), F32)
        for i in range(0, points, 128):
            value = kern_ref[i : i + 128, at] * spread_r[i : i + 128]
            total = total + jnp.sum(value.reshape(16, 8, LANES), axis=0)
        f_ref[:, at] = jnp.sum(total, axis=0, keepdims=True)


def target_body(kern_ref, f0, f1, f2, f3, prior_ref, t_ref, finv_ref, acc):
    points, count = kern_ref.shape
    finv_ref[...] = 1.0 / (four((f0, f1, f2, f3)) + prior_ref[...])
    step = 64
    for i in range(0, points, step):
        total = jnp.zeros((step, LANES), F32)
        for g in range(count // LANES):
            at = slice(g * LANES, (g + 1) * LANES)
            kern = kern_ref[i : i + step, at]
            total = total + kern * kern * finv_ref[:, at]
        acc[i : i + step] = total
    t_ref[...] = jnp.sum(acc[...].T, axis=0, keepdims=True)


def weights(kern, finv, tinv, rinv):
    weight = kern * kern * (kern * finv * tinv - rinv)
    high = weight.astype(BF16)
    return high, (weight - high.astype(F32)).astype(BF16)


def centre_body(kern_ref, rinv_ref, finv_ref, t0, t1, t2, t3, zt_ref, ct_ref, *outs):
    outs, (tinv_ref, ts, rs) = outs[:-3], outs[-3:]
    pieces_x, pieces_h = outs[:SIDE], outs[SIDE:]
    inner = kern_ref.shape[1] // (SIDE * SIDE)
    tinv = 1.0 / four((t0, t1, t2, t3))
    tinv_ref[...] = tinv
    ts[...] = spread(tinv)
    rs[...] = spread(rinv_ref[...])
    place = lax.axis_index("pts") // CORES
    x, h = place // SIDE, place % SIDE
    for s in range(SIDE):
        for t in range(SIDE):
            block = (x ^ s) * SIDE + (h ^ t)
            at = pl.ds(pl.multiple_of(block * inner, inner), inner)
            high, low = weights(
                kern_ref[:, at],
                finv_ref[:, at],
                tile_lanes(ts[...], inner),
                tile_lanes(rs[...], inner),
            )
            sums = jnp.dot(zt_ref[...], high, preferred_element_type=F32) + jnp.dot(
                zt_ref[...], low, preferred_element_type=F32
            )
            grad = sums[:LANES] + sums[LANES : LANES + 1] * ct_ref[:, at]
            pieces_x[s][:, t * inner : (t + 1) * inner] = grad[:ROWS_X]
            pieces_h[t][:, s * inner : (s + 1) * inner] = grad[ROWS_X:]


def embed_body(kern_ref, rinv_ref, finv_ref, tinv_ref, z_ref, zo_ref, c_ref, own, other, ts, rs, acc):
    step = 512
    half = z_ref.shape[0]
    ts[...] = spread(tinv_ref[...])
    rs[...] = spread(rinv_ref[...])
    acc[...] = jnp.zeros_like(acc)

    @pl.loop(0, c_ref.shape[0] // step)
    def _(t):
        at = pl.ds(pl.multiple_of(t * step, step), step)
        high, low = weights(
            kern_ref[:, at],
            finv_ref[:, at],
            tile_lanes(ts[...], step),
            tile_lanes(rs[...], step),
        )
        wide = jnp.concatenate([c_ref[at, :], jnp.ones((step, LANES), BF16)], axis=1)
        acc[...] += jnp.dot(high, wide, preferred_element_type=F32) + jnp.dot(
            low, wide, preferred_element_type=F32
        )

    for base, part, out in ((0, z_ref[...].astype(F32), own), (half, zo_ref[...], other)):
        sums = acc[base : base + half]
        out[...] = SCALE * (sums[:, LANES:] * part - sums[:, :LANES])


def split_body(*refs):
    ins, outs = refs[:SIDE], refs[SIDE:]
    inner = outs[0].shape[1]
    for t in range(SIDE):
        outs[t][...] = four([r.at[:, t * inner : (t + 1) * inner] for r in ins])


def final_body(*refs):
    ins, out = refs[:-1], refs[-1]
    out[...] = jnp.concatenate([four(ins[:SIDE]), four(ins[SIDE:])], axis=0).T


VMEM = pl.BlockSpec(memory_space=pltpu.VMEM)


def call(body, outs, *args, scratch=(), limit=20, name=None, flops=0):
    shapes = tuple(jax.ShapeDtypeStruct(*o) for o in outs)
    moved = sum(a.size * a.dtype.itemsize for a in args)
    return pl.pallas_call(
        body,
        out_shape=shapes,
        in_specs=[VMEM] * len(args),
        out_specs=tuple(VMEM for _ in outs),
        scratch_shapes=scratch,
        compiler_params=pltpu.CompilerParams(vmem_limit_bytes=limit * MIB),
        cost_estimate=pl.CostEstimate(flops=flops, bytes_accessed=moved, transcendentals=0),
        name=name,
    )(*args)


def body(embeddings, centres, prior_freq):
    n_pts, n_ctr = lax.axis_size("pts"), lax.axis_size("ctr")
    half, width = embeddings.shape
    points = CORES * half
    inner = centres.shape[0] // n_pts
    count = centres.shape[0] // CORES
    core = lax.axis_index("pts") % CORES

    def swap_core(v):
        return lax.ppermute(v, "pts", core_perm(n_pts))

    def over_ctr(v):
        other = swap_core(v)
        v = v + jnp.concatenate([other[:, half:], other[:, :half]], axis=1)
        v = v + lax.ppermute(v, "ctr", ctr_perm(n_ctr, SIDE))
        return [v] + [lax.ppermute(v, "ctr", ctr_perm(n_ctr, s)) for s in (1, 2, 3)]

    z_other = swap_core(embeddings.astype(F32))
    own = lax.dynamic_index_in_dim(
        centres.reshape(n_pts // CORES, CORES, inner, width), core, 1, keepdims=False
    ).reshape(count, width)
    prior = lax.dynamic_index_in_dim(
        prior_freq.reshape(n_pts // CORES, CORES, inner), core, 1, keepdims=False
    ).reshape(1, count)

    kern, row, ct, zt = call(
        kern_body,
        [((points, count), F32), ((1, points), F32), ((width, count), F32), ((width + ONES, points), BF16)],
        embeddings,
        z_other,
        own,
        scratch=[
            pltpu.VMEM((points, width), BF16),
            pltpu.VMEM((points, LANES), F32),
            pltpu.VMEM((points, LANES), F32),
        ],
        name="kern",
    )
    freq, rinv = call(
        freq_body, [((1, count), F32), ((1, points), F32)], kern, *over_ctr(row), name="freq"
    )
    freq = [freq] + [lax.ppermute(freq, "pts", x_perm(n_pts, s)) for s in (1, 2, 3)]
    freq = (freq[0] + freq[1]) + (freq[2] + freq[3])
    freq = [freq] + [lax.ppermute(freq, "pts", h_perm(n_pts, s)) for s in (1, 2, 3)]
    target, finv = call(
        target_body,
        [((1, points), F32), ((1, count), F32)],
        kern,
        *freq,
        prior,
        scratch=[pltpu.VMEM((points, LANES), F32)],
        name="target",
    )
    spreads = [pltpu.VMEM((points, LANES), F32)] * 2
    *pieces, tinv = call(
        centre_body,
        [((ROWS_X, SIDE * inner), F32)] * SIDE
        + [((width - ROWS_X, SIDE * inner), F32)] * SIDE
        + [((1, points), F32)],
        kern,
        rinv,
        finv,
        *over_ctr(target),
        zt,
        ct,
        scratch=spreads,
        name="centre",
    )
    by_x, by_h = pieces[:SIDE], pieces[SIDE:]
    by_x = [by_x[0]] + [lax.ppermute(by_x[s], "pts", x_perm(n_pts, s)) for s in (1, 2, 3)]
    by_h = [by_h[0]] + [lax.ppermute(by_h[s], "pts", h_perm(n_pts, s)) for s in (1, 2, 3)]
    mine, other = call(
        embed_body,
        [((half, width), F32)] * 2,
        kern,
        rinv,
        finv,
        tinv,
        embeddings,
        z_other,
        own,
        scratch=spreads + [pltpu.VMEM((points, 2 * LANES), F32)],
        name="embed",
    )
    embed = mine + swap_core(other)
    for s in (SIDE, 1, 3):
        embed = embed + lax.ppermute(embed, "ctr", ctr_perm(n_ctr, s))

    by_x = call(split_body, [((ROWS_X, inner), F32)] * SIDE, *by_x, name="split_x")
    by_h = call(split_body, [((width - ROWS_X, inner), F32)] * SIDE, *by_h, name="split_h")
    by_x = [by_x[0]] + [lax.ppermute(by_x[s], "pts", h_perm(n_pts, s)) for s in (1, 2, 3)]
    by_h = [by_h[0]] + [lax.ppermute(by_h[s], "pts", x_perm(n_pts, s)) for s in (1, 2, 3)]
    (grad,) = call(final_body, [((inner, width), F32)], *by_x, *by_h, name="final")
    return embed, grad.reshape(1, inner, width)


def solution(mesh):
    in_specs = (P("pts", None), P("ctr", None), P("ctr"))
    out_specs = (P("pts", None), P("ctr", "pts", None))
    return jax.shard_map(body, mesh=mesh, in_specs=in_specs, out_specs=out_specs, check_vma=False)
```

time: 483 us -> 135 us (0.28)
  blocking collectives: 177 us -> 0 us
  matrix products: 140 us -> 0 us
  starting transfers between devices: 0.08 us -> 51 us
  other arithmetic: 51.7 us -> 3.42 us
  waiting for transfers between devices: 90.2 us -> 48.2 us
  Pallas kernels: 0 us -> 20.9 us
  between operations: 15.6 us -> 0.9 us
  local copies, waits for them, and re-layouts: 2.84 us -> 10.7 us
    psum x3 -> x0, blocking collectives: 177 us -> none  [the longest x1 142 us: body(): freqs = lax.psum(lax.map(freq_part, blocks), 'pts') + priors]
    dot_general x56 -> x0, matrix products: 140 us -> none  [the longest x40 75.9 us: kernel(): cross = jnp.dot(points, block.T, preferred_element_type=jnp.float32)]
    reduce_scatter x1 -> x0, waiting for transfers between devices: 87.5 us -> none  [body(): lax.psum_scatter(lax.map(centre_block, (sub_blocks, sub_freqs)).reshape(r...]
    ppermute x0 -> x33, starting transfers between devices: none -> 51 us  [the longest x6 8.19 us: over_ctr(): return [v] + [lax.ppermute(v, 'ctr', ctr_perm(n_ctr, s)) for s in (1, 2, 3)]]
    ppermute x0 -> x33, waiting for transfers between devices: none -> 48.2 us  [the longest x3 10.5 us: body(): lax.ppermute(by_h[s], 'pts', h_perm(n_pts, s))]
    reduce_sum x43 -> x0, other arithmetic: 47.5 us -> none  [the longest x40 46.4 us: kernel(): block_norms = jnp.sum(jnp.square(block.astype(jnp.float32)), axis=1)]
    pallas_call x0 -> x8, Pallas kernels: none -> 20.9 us  [call(): pl.pallas_call(body, out_shape=shapes, in_specs=[VMEM] * len(args), out_s...]
    unnamed x4 -> x28, local copies, waits for them, and re-layouts: 0.7 us -> 8.49 us
  transfers between devices with their start and end apart: 2 -> 33, of which waited for: 2 -> 17; matrix products, arithmetic and copies ran while one was open for 15% -> 2% of each run, Pallas kernels for 0% -> 1%
where the time goes in v1:
time: 135 us
  starting transfers between devices  51 us (38%)
  waiting for transfers between devices  48.2 us (36%)
  Pallas kernels  20.9 us (15%)
  local copies, waits for them, and re-layouts  10.7 us (8%)
  other arithmetic  3.42 us (3%)
    pallas_call x8, Pallas kernels, call(): pl.pallas_call(body, out_shape=shapes, in_specs=[VMEM] * len(args), out_s...  20.9 us
    ppermute x3, waiting for transfers between devices, body(): lax.ppermute(by_h[s], 'pts', h_perm(n_pts, s))  10.5 us
    unnamed x28, local copies, waits for them, and re-layouts  8.49 us
    ppermute x6, starting transfers between devices, over_ctr(): return [v] + [lax.ppermute(v, 'ctr', ctr_perm(n_ctr, s)) for s in (1, 2, 3)]  8.19 us
    ppermute x3, waiting for transfers between devices, body(): embed = embed + lax.ppermute(embed, 'ctr', ctr_perm(n_ctr, s))  8 us
    ppermute x3, starting transfers between devices, body(): lax.ppermute(by_h[s], 'pts', h_perm(n_pts, s))  7.98 us
    ppermute x3, starting transfers between devices, body(): lax.ppermute(freq, 'pts', h_perm(n_pts, s))  7.95 us
    ppermute x3, starting transfers between devices, body(): lax.ppermute(by_x[s], 'pts', h_perm(n_pts, s))  6.58 us
  transfers between devices with their start and end apart: 33, of which 17 were waited for; matrix products, arithmetic and copies ran while one was open for 2% of the time, Pallas kernels for 1%

profile of v1, /device:TPU:32, one launch (start us, length us, event | category | flops | bytes accessed | tf_op | source)
XLA Modules:
  0.0 135.2 jit_solution(10753818976030264258)
XLA Ops:
  4.2 4.7 %kern.1 = (f32[1024,4096]{1,0:T(8,128)S(1)}, f32[1,1024]{1,0:T(1,128)S(1)}, f32[128,4096]{1,0:T(8,128)S(1)}, bf16[144,1024]{1,0:T(8,128)(2,1)S(1)}) custom-call(bf16[512,128]{1,0:T(8,128)(2,1)S(1)} %copy-done.5, f32[512,128]{1,0:T(8,128)S(1)} %collective-permute-done.zo_ref, bf16[4096,128]{1,0:T(8,128)(2,1)S(1)} %bitcast.9), custom_call_target="tpu_custom_call" | custom-call | bytes 1441792 | tf_op jit(solution)/shard_map/kern/pallas_call | solution.py:183
  12.1 1.9 %collective-permute-start.2 = (f32[1,1024]{1,0:T(1,128)S(1)}, f32[1,1024]{1,0:T(1,128)S(1)}, u32[]{:S(2)}, u32[]{:S(2)}) collective-permute-start(f32[1,1024]{1,0:T(1,128)S(1)} %maximum_add_fusion), channel_id=1, source_target_pairs={{0,4},{1,5},{2,6},{3,7},{4,0},{5,1},{6,2},{7,3},{8,12},{9,13},{10,... | collective-permute-start | bytes 12296 | tf_op jit(solution)/shard_map/ppermute | solution.py:209
  15.8 3.0 %collective-permute-start.5 = (f32[1,1024]{1,0:T(1,128)S(1)}, f32[1,1024]{1,0:T(1,128)S(1)}, u32[]{:S(2)}, u32[]{:S(2)}) collective-permute-start(f32[1,1024]{1,0:T(1,128)S(1)} %add.46.r0), channel_id=1, source_target_pairs={{0,3},{1,2},{2,1},{3,0},{4,7},{5,6},{6,5},{7,4},{8,11},{9,10},{10,... | collective-permute-start | bytes 12296 | tf_op jit(solution)/shard_map/ppermute | solution.py:210
  20.7 3.3 %collective-permute-done.4.r2 = f32[1,1024]{1,0:T(1,128)S(1)} collective-permute-done((f32[1,1024]{1,0:T(1,128)S(1)}, f32[1,1024]{1,0:T(1,128)S(1)}, u32[]{:S(2)}, u32[]{:S(2)}) %collective-permute-start.4) | collective-permute-done | bytes 4128 | tf_op jit(solution)/shard_map/ppermute | solution.py:210
  26.0 2.8 %collective-permute-start.8 = (f32[1,4096]{1,0:T(1,128)S(1)}, f32[1,4096]{1,0:T(1,128)}, u32[]{:S(2)}, u32[]{:S(2)}) collective-permute-start(f32[1,4096]{1,0:T(1,128)S(1)} %get-tuple-element.32), channel_id=1, source_target_pairs={{0,192},{8,200},{16,208},{24,216},{32,224},{40,232},{48,240},{56,2... | collective-permute-start | bytes 49160 | tf_op jit(solution)/shard_map/ppermute | solution.py:236
  31.5 2.6 %collective-permute-done.7 = f32[1,4096]{1,0:T(1,128)} collective-permute-done((f32[1,4096]{1,0:T(1,128)S(1)}, f32[1,4096]{1,0:T(1,128)}, u32[]{:S(2)}, u32[]{:S(2)}) %collective-permute-start.7) | collective-permute-done | bytes 16416 | tf_op jit(solution)/shard_map/ppermute | solution.py:236
  34.9 5.5 %collective-permute-start.11 = (f32[1,4096]{1,0:T(1,128)S(1)}, f32[1,4096]{1,0:T(1,128)S(1)}, u32[]{:S(2)}, u32[]{:S(2)}) collective-permute-start(f32[1,4096]{1,0:T(1,128)S(1)} %add_add_fusion.f0), channel_id=1, source_target_pairs={{0,48},{8,56},{16,32},{24,40},{32,16},{40,24},{48,0},{56,8},{64,11... | collective-permute-start | bytes 49160 | tf_op jit(solution)/shard_map/ppermute | solution.py:238
  43.6 4.4 %collective-permute-done.10.f2 = f32[1,4096]{1,0:T(1,128)S(1)} collective-permute-done((f32[1,4096]{1,0:T(1,128)S(1)}, f32[1,4096]{1,0:T(1,128)S(1)}, u32[]{:S(2)}, u32[]{:S(2)}) %collective-permute-start.10) | collective-permute-done | bytes 16416 | tf_op jit(solution)/shard_map/ppermute | solution.py:238
  48.0 5.8 %copy-done.2 = f32[1024,4096]{1,0:T(8,128)S(1)} copy-done((f32[1024,4096]{1,0:T(8,128)S(1)}, f32[1024,4096]{1,0:T(8,128)}, u32[]{:S(2)}) %copy-start.2) | copy-done | bytes 16777240
  58.1 2.6 %collective-permute-done.13 = f32[1,1024]{1,0:T(1,128)S(1)} collective-permute-done((f32[1,1024]{1,0:T(1,128)S(1)}, f32[1,1024]{1,0:T(1,128)S(1)}, u32[]{:S(2)}, u32[]{:S(2)}) %collective-permute-start.13) | collective-permute-done | bytes 4128 | tf_op jit(solution)/shard_map/ppermute | solution.py:209
  62.9 1.9 %collective-permute-start.14 = (f32[1,1024]{1,0:T(1,128)S(1)}, f32[1,1024]{1,0:T(1,128)S(1)}, u32[]{:S(2)}, u32[]{:S(2)}) collective-permute-start(f32[1,1024]{1,0:T(1,128)S(1)} %add.51.t0), channel_id=1, source_target_pairs={{0,1},{1,0},{2,3},{3,2},{4,5},{5,4},{6,7},{7,6},{8,9},{9,8},{10,11... | collective-permute-start | bytes 12296 | tf_op jit(solution)/shard_map/ppermute | solution.py:210
  67.1 5.6 %centre.1 = (f32[88,1024]{1,0:T(8,128)S(1)}, f32[88,1024]{1,0:T(8,128)S(1)}, f32[88,1024]{1,0:T(8,128)S(1)}, f32[88,1024]{1,0:T(8,128)S(1)}, f32[40,1024]{1,0:T(...) custom-call(f32[1024,4096]{1,0:T(8,128)S(1)} %copy-done.2, ...), custom_call_target="tpu_custom_call" | custom-call | bytes 19206144 | tf_op jit(solution)/shard_map/centre/pallas_call | solution.py:183
  72.8 6.6 %embed.1 = (f32[512,128]{1,0:T(8,128)S(1)}, f32[512,128]{1,0:T(8,128)S(1)}) custom-call(f32[1024,4096]{1,0:T(8,128)S(1)} %bitcast.8, f32[1,1024]{1,0:T(1,128)S(1)} %copy-done.9, f32[1,4096]{1,0:T(1,128)S(1)} %get-tuple-element.33.finv_ref, f32[1,1024]{1,0:T(1,128)S(1)} %get-tuple-element.37.tinv_ref, bf16[512,128]{1,0:T(8,128)(2,1)S(1)} %copy-done.5, ...), custom_call_target="tpu_custom_call" | custom-call | bytes 18243584 | tf_op jit(solution)/shard_map/embed/pallas_call | solution.py:183
  83.6 8.0 %collective-permute-done.18 = f32[512,128]{1,0:T(8,128)S(1)} collective-permute-done((f32[512,128]{1,0:T(8,128)S(1)}, f32[512,128]{1,0:T(8,128)S(1)}, u32[]{:S(2)}, u32[]{:S(2)}) %collective-permute-start.18) | collective-permute-done | bytes 262176 | tf_op jit(solution)/shard_map/ppermute | solution.py:281
  93.2 2.6 %collective-permute-start.22 = (f32[88,1024]{1,0:T(8,128)S(1)}, f32[88,1024]{1,0:T(8,128)S(1)}, u32[]{:S(2)}, u32[]{:S(2)}) collective-permute-start(f32[88,1024]{1,0:T(8,128)S(1)} %get-tuple-element.42), channel_id=1, source_target_pairs={{0,128},{8,136},{16,144},{24,152},{32,160},{40,168},{48,176},{56,1... | collective-permute-start | bytes 1081352 | tf_op jit(solution)/shard_map/ppermute | solution.py:264
  97.6 2.9 %collective-permute-start.28 = (f32[40,1024]{1,0:T(8,128)S(1)}, f32[40,1024]{1,0:T(8,128)S(1)}, u32[]{:S(2)}, u32[]{:S(2)}) collective-permute-start(f32[40,1024]{1,0:T(8,128)S(1)} %get-tuple-element.50), channel_id=1, source_target_pairs={{0,32},{8,40},{16,48},{24,56},{32,0},{40,8},{48,16},{56,24},{64,96... | collective-permute-start | bytes 491528 | tf_op jit(solution)/shard_map/ppermute | solution.py:265
  100.6 3.7 %collective-permute-start.29 = (f32[40,1024]{1,0:T(8,128)S(1)}, f32[40,1024]{1,0:T(8,128)S(1)}, u32[]{:S(2)}, u32[]{:S(2)}) collective-permute-start(f32[40,1024]{1,0:T(8,128)S(1)} %get-tuple-element.51), channel_id=1, source_target_pairs={{0,48},{8,56},{16,32},{24,40},{32,16},{40,24},{48,0},{56,8},{64,11... | collective-permute-start | bytes 491528 | tf_op jit(solution)/shard_map/ppermute | solution.py:265
  104.3 4.8 %collective-permute-done.28.refs_2_ = f32[40,1024]{1,0:T(8,128)S(1)} collective-permute-done((f32[40,1024]{1,0:T(8,128)S(1)}, f32[40,1024]{1,0:T(8,128)S(1)}, u32[]{:S(2)}, u32[]{:S(2)}) %collective-permute-start.28) | collective-permute-done | bytes 163872 | tf_op jit(solution)/shard_map/ppermute | solution.py:265
  110.4 5.7 %collective-permute-done.29.refs_3_ = f32[40,1024]{1,0:T(8,128)S(1)} collective-permute-done((f32[40,1024]{1,0:T(8,128)S(1)}, f32[40,1024]{1,0:T(8,128)S(1)}, u32[]{:S(2)}, u32[]{:S(2)}) %collective-permute-start.29) | collective-permute-done | bytes 163872 | tf_op jit(solution)/shard_map/ppermute | solution.py:265
  116.7 2.7 %collective-permute-start.25 = (f32[88,256]{1,0:T(8,128)S(1)}, f32[88,256]{1,0:T(8,128)S(1)}, u32[]{:S(2)}, u32[]{:S(2)}) collective-permute-start(f32[88,256]{1,0:T(8,128)S(1)} %get-tuple-element.46), channel_id=1, source_target_pairs={{0,32},{8,40},{16,48},{24,56},{32,0},{40,8},{48,16},{56,24},{64,96... | collective-permute-start | bytes 270344 | tf_op jit(solution)/shard_map/ppermute | solution.py:285
  119.4 3.5 %collective-permute-start.26 = (f32[88,256]{1,0:T(8,128)S(1)}, f32[88,256]{1,0:T(8,128)S(1)}, u32[]{:S(2)}, u32[]{:S(2)}) collective-permute-start(f32[88,256]{1,0:T(8,128)S(1)} %get-tuple-element.47), channel_id=1, source_target_pairs={{0,48},{8,56},{16,32},{24,40},{32,16},{40,24},{48,0},{56,8},{64,11... | collective-permute-start | bytes 270344 | tf_op jit(solution)/shard_map/ppermute | solution.py:285
  122.9 2.8 %collective-permute-start.31 = (f32[40,256]{1,0:T(8,128)S(1)}, f32[40,256]{1,0:T(8,128)S(1)}, u32[]{:S(2)}, u32[]{:S(2)}) collective-permute-start(f32[40,256]{1,0:T(8,128)S(1)} %get-tuple-element.54), channel_id=1, source_target_pairs={{0,128},{8,136},{16,144},{24,152},{32,160},{40,168},{48,176},{56,1... | collective-permute-start | bytes 122888 | tf_op jit(solution)/shard_map/ppermute | solution.py:286
  125.7 2.7 %collective-permute-done.31.refs_6_ = f32[40,256]{1,0:T(8,128)S(1)} collective-permute-done((f32[40,256]{1,0:T(8,128)S(1)}, f32[40,256]{1,0:T(8,128)S(1)}, u32[]{:S(2)}, u32[]{:S(2)}) %collective-permute-start.31) | collective-permute-done | bytes 40992 | tf_op jit(solution)/shard_map/ppermute | solution.py:286
  129.8 3.8 %collective-permute-done.32.refs_7_ = f32[40,256]{1,0:T(8,128)S(1)} collective-permute-done((f32[40,256]{1,0:T(8,128)S(1)}, f32[40,256]{1,0:T(8,128)S(1)}, u32[]{:S(2)}, u32[]{:S(2)}) %collective-permute-start.32) | collective-permute-done | bytes 40992 | tf_op jit(solution)/shard_map/ppermute | solution.py:286
  (94 shorter events, 40.3 us)
Async XLA Ops:
  15.8 4.8 %collective-permute-start.5 = (f32[1,1024]{1,0:T(1,128)S(1)}, f32[1,1024]{1,0:T(1,128)S(1)}, u32[]{:S(2)}, u32[]{:S(2)}) collective-permute-start(f32[1,1024]{1,0:T(1,128)S(1)} %add.46.r0), channel_id=1, source_target_pairs={{0,3},{1,2},{2,1},{3,0},{4,7},{5,6},{6,5},{7,4},{8,11},{9,10},{10,... | collective-permute-start | bytes 12296 | tf_op jit(solution)/shard_map/ppermute | solution.py:210
  18.9 5.1 %collective-permute-start.4 = (f32[1,1024]{1,0:T(1,128)S(1)}, f32[1,1024]{1,0:T(1,128)S(1)}, u32[]{:S(2)}, u32[]{:S(2)}) collective-permute-start(f32[1,1024]{1,0:T(1,128)S(1)} %add.46.r0), channel_id=1, source_target_pairs={{0,2},{1,3},{2,0},{3,1},{4,6},{5,7},{6,4},{7,5},{8,10},{9,11},{10,... | collective-permute-start | bytes 12296 | tf_op jit(solution)/shard_map/ppermute | solution.py:210
  26.0 5.5 %collective-permute-start.8 = (f32[1,4096]{1,0:T(1,128)S(1)}, f32[1,4096]{1,0:T(1,128)}, u32[]{:S(2)}, u32[]{:S(2)}) collective-permute-start(f32[1,4096]{1,0:T(1,128)S(1)} %get-tuple-element.32), channel_id=1, source_target_pairs={{0,192},{8,200},{16,208},{24,216},{32,224},{40,232},{48,240},{56,2... | collective-permute-start | bytes 49160 | tf_op jit(solution)/shard_map/ppermute | solution.py:236
  28.8 5.3 %collective-permute-start.7 = (f32[1,4096]{1,0:T(1,128)S(1)}, f32[1,4096]{1,0:T(1,128)}, u32[]{:S(2)}, u32[]{:S(2)}) collective-permute-start(f32[1,4096]{1,0:T(1,128)S(1)} %get-tuple-element.32), channel_id=1, source_target_pairs={{0,128},{8,136},{16,144},{24,152},{32,160},{40,168},{48,176},{56,1... | collective-permute-start | bytes 49160 | tf_op jit(solution)/shard_map/ppermute | solution.py:236
  34.9 8.7 %collective-permute-start.11 = (f32[1,4096]{1,0:T(1,128)S(1)}, f32[1,4096]{1,0:T(1,128)S(1)}, u32[]{:S(2)}, u32[]{:S(2)}) collective-permute-start(f32[1,4096]{1,0:T(1,128)S(1)} %add_add_fusion.f0), channel_id=1, source_target_pairs={{0,48},{8,56},{16,32},{24,40},{32,16},{40,24},{48,0},{56,8},{64,11... | collective-permute-start | bytes 49160 | tf_op jit(solution)/shard_map/ppermute | solution.py:238
  40.4 7.6 %collective-permute-start.10 = (f32[1,4096]{1,0:T(1,128)S(1)}, f32[1,4096]{1,0:T(1,128)S(1)}, u32[]{:S(2)}, u32[]{:S(2)}) collective-permute-start(f32[1,4096]{1,0:T(1,128)S(1)} %add_add_fusion.f0), channel_id=1, source_target_pairs={{0,32},{8,40},{16,48},{24,56},{32,0},{40,8},{48,16},{56,24},{64,96... | collective-permute-start | bytes 49160 | tf_op jit(solution)/shard_map/ppermute | solution.py:238
  41.8 6.2 %collective-permute-start.9 = (f32[1,4096]{1,0:T(1,128)S(1)}, f32[1,4096]{1,0:T(1,128)S(1)}, u32[]{:S(2)}, u32[]{:S(2)}) collective-permute-start(f32[1,4096]{1,0:T(1,128)S(1)} %add_add_fusion.f0), channel_id=1, source_target_pairs={{0,16},{8,24},{16,0},{24,8},{32,48},{40,56},{48,32},{56,40},{64,80... | collective-permute-start | bytes 49160 | tf_op jit(solution)/shard_map/ppermute | solution.py:238
  60.7 4.8 %collective-permute-start.16 = (f32[1,1024]{1,0:T(1,128)S(1)}, f32[1,1024]{1,0:T(1,128)S(1)}, u32[]{:S(2)}, u32[]{:S(2)}) collective-permute-start(f32[1,1024]{1,0:T(1,128)S(1)} %add.51.t0), channel_id=1, source_target_pairs={{0,3},{1,2},{2,1},{3,0},{4,7},{5,6},{6,5},{7,4},{8,11},{9,10},{10,... | collective-permute-start | bytes 12296 | tf_op jit(solution)/shard_map/ppermute | solution.py:210
  62.0 5.1 %collective-permute-start.15 = (f32[1,1024]{1,0:T(1,128)S(1)}, f32[1,1024]{1,0:T(1,128)S(1)}, u32[]{:S(2)}, u32[]{:S(2)}) collective-permute-start(f32[1,1024]{1,0:T(1,128)S(1)} %add.51.t0), channel_id=1, source_target_pairs={{0,2},{1,3},{2,0},{3,1},{4,6},{5,7},{6,4},{7,5},{8,10},{9,11},{10,... | collective-permute-start | bytes 12296 | tf_op jit(solution)/shard_map/ppermute | solution.py:210
  81.1 10.5 %collective-permute-start.18 = (f32[512,128]{1,0:T(8,128)S(1)}, f32[512,128]{1,0:T(8,128)S(1)}, u32[]{:S(2)}, u32[]{:S(2)}) collective-permute-start(f32[512,128]{1,0:T(8,128)S(1)} %add.52), channel_id=1, source_target_pairs={{0,4},{1,5},{2,6},{3,7},{4,0},{5,1},{6,2},{7,3},{8,12},{9,13},{10,... | collective-permute-start | bytes 786440 | tf_op jit(solution)/shard_map/ppermute | solution.py:281
  82.2 15.5 %collective-permute-start.27 = (f32[40,1024]{1,0:T(8,128)S(1)}, f32[40,1024]{1,0:T(8,128)S(1)}, u32[]{:S(2)}, u32[]{:S(2)}) collective-permute-start(f32[40,1024]{1,0:T(8,128)S(1)} %get-tuple-element.49), channel_id=1, source_target_pairs={{0,16},{8,24},{16,0},{24,8},{32,48},{40,56},{48,32},{56,40},{64,80... | collective-permute-start | bytes 491528 | tf_op jit(solution)/shard_map/ppermute | solution.py:265
  91.6 9.0 %collective-permute-start.19 = (f32[512,128]{1,0:T(8,128)S(1)}, f32[512,128]{1,0:T(8,128)S(1)}, u32[]{:S(2)}, u32[]{:S(2)}) collective-permute-start(f32[512,128]{1,0:T(8,128)S(1)} %add.53), channel_id=1, source_target_pairs={{0,1},{1,0},{2,3},{3,2},{4,5},{5,4},{6,7},{7,6},{8,9},{9,8},{10,11... | collective-permute-start | bytes 786440 | tf_op jit(solution)/shard_map/ppermute | solution.py:281
  92.9 23.3 %collective-permute-start.21 = (f32[88,1024]{1,0:T(8,128)S(1)}, f32[88,1024]{1,0:T(8,128)S(1)}, u32[]{:S(2)}, u32[]{:S(2)}) collective-permute-start(f32[88,1024]{1,0:T(8,128)S(1)} %get-tuple-element.41), channel_id=1, source_target_pairs={{0,64},{8,72},{16,80},{24,88},{32,96},{40,104},{48,112},{56,120},{... | collective-permute-start | bytes 1081352 | tf_op jit(solution)/shard_map/ppermute | solution.py:264
  93.2 23.1 %collective-permute-start.22 = (f32[88,1024]{1,0:T(8,128)S(1)}, f32[88,1024]{1,0:T(8,128)S(1)}, u32[]{:S(2)}, u32[]{:S(2)}) collective-permute-start(f32[88,1024]{1,0:T(8,128)S(1)} %get-tuple-element.42), channel_id=1, source_target_pairs={{0,128},{8,136},{16,144},{24,152},{32,160},{40,168},{48,176},{56,1... | collective-permute-start | bytes 1081352 | tf_op jit(solution)/shard_map/ppermute | solution.py:264
  95.8 20.5 %collective-permute-start.23 = (f32[88,1024]{1,0:T(8,128)S(1)}, f32[88,1024]{1,0:T(8,128)S(1)}, u32[]{:S(2)}, u32[]{:S(2)}) collective-permute-start(f32[88,1024]{1,0:T(8,128)S(1)} %get-tuple-element.43), channel_id=1, source_target_pairs={{0,192},{8,200},{16,208},{24,216},{32,224},{40,232},{48,240},{56,2... | collective-permute-start | bytes 1081352 | tf_op jit(solution)/shard_map/ppermute | solution.py:264
  97.6 11.5 %collective-permute-start.28 = (f32[40,1024]{1,0:T(8,128)S(1)}, f32[40,1024]{1,0:T(8,128)S(1)}, u32[]{:S(2)}, u32[]{:S(2)}) collective-permute-start(f32[40,1024]{1,0:T(8,128)S(1)} %get-tuple-element.50), channel_id=1, source_target_pairs={{0,32},{8,40},{16,48},{24,56},{32,0},{40,8},{48,16},{56,24},{64,96... | collective-permute-start | bytes 491528 | tf_op jit(solution)/shard_map/ppermute | solution.py:265
  100.6 15.5 %collective-permute-start.29 = (f32[40,1024]{1,0:T(8,128)S(1)}, f32[40,1024]{1,0:T(8,128)S(1)}, u32[]{:S(2)}, u32[]{:S(2)}) collective-permute-start(f32[40,1024]{1,0:T(8,128)S(1)} %get-tuple-element.51), channel_id=1, source_target_pairs={{0,48},{8,56},{16,32},{24,40},{32,16},{40,24},{48,0},{56,8},{64,11... | collective-permute-start | bytes 491528 | tf_op jit(solution)/shard_map/ppermute | solution.py:265
  109.1 25.3 %collective-permute-start.20 = (f32[512,128]{1,0:T(8,128)S(1)}, f32[512,128]{1,0:T(8,128)S(1)}, u32[]{:S(2)}, u32[]{:S(2)}) collective-permute-start(f32[512,128]{1,0:T(8,128)S(1)} %add.54), channel_id=1, source_target_pairs={{0,3},{1,2},{2,1},{3,0},{4,7},{5,6},{6,5},{7,4},{8,11},{9,10},{10,... | collective-permute-start | bytes 786440 | tf_op jit(solution)/shard_map/ppermute | solution.py:281
  116.1 6.8 %collective-permute-start.30 = (f32[40,256]{1,0:T(8,128)S(1)}, f32[40,256]{1,0:T(8,128)S(1)}, u32[]{:S(2)}, u32[]{:S(2)}) collective-permute-start(f32[40,256]{1,0:T(8,128)S(1)} %get-tuple-element.53), channel_id=1, source_target_pairs={{0,64},{8,72},{16,80},{24,88},{32,96},{40,104},{48,112},{56,120},{... | collective-permute-start | bytes 122888 | tf_op jit(solution)/shard_map/ppermute | solution.py:286
  116.3 17.3 %collective-permute-start.24 = (f32[88,256]{1,0:T(8,128)S(1)}, f32[88,256]{1,0:T(8,128)S(1)}, u32[]{:S(2)}, u32[]{:S(2)}) collective-permute-start(f32[88,256]{1,0:T(8,128)S(1)} %get-tuple-element.45), channel_id=1, source_target_pairs={{0,16},{8,24},{16,0},{24,8},{32,48},{40,56},{48,32},{56,40},{64,80... | collective-permute-start | bytes 270344 | tf_op jit(solution)/shard_map/ppermute | solution.py:285
  116.7 17.0 %collective-permute-start.25 = (f32[88,256]{1,0:T(8,128)S(1)}, f32[88,256]{1,0:T(8,128)S(1)}, u32[]{:S(2)}, u32[]{:S(2)}) collective-permute-start(f32[88,256]{1,0:T(8,128)S(1)} %get-tuple-element.46), channel_id=1, source_target_pairs={{0,32},{8,40},{16,48},{24,56},{32,0},{40,8},{48,16},{56,24},{64,96... | collective-permute-start | bytes 270344 | tf_op jit(solution)/shard_map/ppermute | solution.py:285
  119.4 14.2 %collective-permute-start.26 = (f32[88,256]{1,0:T(8,128)S(1)}, f32[88,256]{1,0:T(8,128)S(1)}, u32[]{:S(2)}, u32[]{:S(2)}) collective-permute-start(f32[88,256]{1,0:T(8,128)S(1)} %get-tuple-element.47), channel_id=1, source_target_pairs={{0,48},{8,56},{16,32},{24,40},{32,16},{40,24},{48,0},{56,8},{64,11... | collective-permute-start | bytes 270344 | tf_op jit(solution)/shard_map/ppermute | solution.py:285
  122.9 5.5 %collective-permute-start.31 = (f32[40,256]{1,0:T(8,128)S(1)}, f32[40,256]{1,0:T(8,128)S(1)}, u32[]{:S(2)}, u32[]{:S(2)}) collective-permute-start(f32[40,256]{1,0:T(8,128)S(1)} %get-tuple-element.54), channel_id=1, source_target_pairs={{0,128},{8,136},{16,144},{24,152},{32,160},{40,168},{48,176},{56,1... | collective-permute-start | bytes 122888 | tf_op jit(solution)/shard_map/ppermute | solution.py:286
  128.4 5.2 %collective-permute-start.32 = (f32[40,256]{1,0:T(8,128)S(1)}, f32[40,256]{1,0:T(8,128)S(1)}, u32[]{:S(2)}, u32[]{:S(2)}) collective-permute-start(f32[40,256]{1,0:T(8,128)S(1)} %get-tuple-element.55), channel_id=1, source_target_pairs={{0,192},{8,200},{16,208},{24,216},{32,224},{40,232},{48,240},{56,2... | collective-permute-start | bytes 122888 | tf_op jit(solution)/shard_map/ppermute | solution.py:286
  (23 other events, 143.9 us)

commit v2 on v1

v2 whole, which is shorter than its diff:
```python
import jax
import jax.numpy as jnp
from jax import lax
from jax.experimental import pallas as pl
from jax.experimental.pallas import tpu as pltpu
from jax.sharding import PartitionSpec as P

SIDE = 4
CORES = 2
LANES = 128
ONES = 16
SCALE = 128.0
ROWS_X = 88
MIB = 2**20
F32 = jnp.float32
BF16 = jnp.bfloat16


def core_perm(size):
    return [(i, i ^ 1) for i in range(size)]


def x_perm(size, s):
    return [(i, i ^ (s * SIDE * CORES)) for i in range(size)]


def h_perm(size, s):
    return [(i, i ^ (s * CORES)) for i in range(size)]


def ctr_perm(size, s):
    return [(i, i ^ s) for i in range(size)]


def tile_lanes(column, width):
    return jnp.concatenate([column] * (width // LANES), axis=1)


def spread(row):
    return jnp.broadcast_to(row, (LANES, row.shape[1])).T


def four(refs):
    a, b, c, d = refs
    return (a[...] + b[...]) + (c[...] + d[...])


def block_rows(block, inner, core):
    return pl.ds(pl.multiple_of((block * CORES + core) * inner, inner), inner)


def kern_part(part, c_ref, kern_ref, za, zn):
    points = part.shape[0]
    inner = c_ref.shape[0] // lax.axis_size("pts")
    core = lax.axis_index("pts") % CORES
    zn[...] = jnp.broadcast_to(jnp.sum(part * part, axis=1, keepdims=True) + 1.0, (points, LANES))
    za[...] = (-2.0 * part).astype(BF16)
    total = jnp.zeros((points, LANES), F32)
    for block in range(kern_ref.shape[1] // inner):
        ct = c_ref[block_rows(block, inner, core), :].astype(F32).T
        norms = jnp.sum(ct * ct, axis=0, keepdims=True)
        cross = jnp.dot(za[...], ct.astype(BF16), preferred_element_type=F32)
        kern = 1.0 / (cross + norms + tile_lanes(zn[...], inner))
        kern_ref[:, block * inner : (block + 1) * inner] = kern
        for g in range(inner // LANES):
            total = total + kern[:, g * LANES : (g + 1) * LANES]
    return jnp.sum(total.T, axis=0, keepdims=True)


def own_body(z_ref, c_ref, kern_ref, row_ref, za, zn):
    row_ref[...] = kern_part(z_ref[...].astype(F32), c_ref, kern_ref, za, zn)


def other_body(zo_ref, c_ref, row_ref, kern_ref, rows_ref, za, zn):
    rows_ref[:1] = row_ref[...]
    rows_ref[1:] = kern_part(zo_ref[...], c_ref, kern_ref, za, zn)


def swap_add_body(mine, theirs, out):
    out[:1] = mine[:1] + theirs[1:]
    out[1:] = mine[1:] + theirs[:1]


def add_body(*refs):
    refs[-1][...] = four(refs[:-1]) if len(refs) == 5 else refs[0][...] + refs[1][...]


def freq_body(own_ref, other_ref, r0, r1, r2, r3, f_ref, rinv_ref):
    half, count = own_ref.shape
    rinv = 1.0 / four((r0, r1, r2, r3))
    rinv_ref[...] = rinv
    parts = ((own_ref, spread(rinv[:1])), (other_ref, spread(rinv[1:])))
    for g in range(count // LANES):
        at = slice(g * LANES, (g + 1) * LANES)
        total = jnp.zeros((8, LANES), F32)
        for kern_ref, scale in parts:
            for i in range(0, half, 128):
                value = kern_ref[i : i + 128, at] * scale[i : i + 128]
                total = total + jnp.sum(value.reshape(16, 8, LANES), axis=0)
        f_ref[:, at] = jnp.sum(total, axis=0, keepdims=True)


def target_body(own_ref, other_ref, f0, f1, f2, f3, prior_ref, t_ref, finv_ref, acc):
    half, count = own_ref.shape
    inner = prior_ref.shape[1] // lax.axis_size("pts")
    core = lax.axis_index("pts") % CORES
    prior = [prior_ref[:, block_rows(b, inner, core)] for b in range(count // inner)]
    finv_ref[...] = 1.0 / (four((f0, f1, f2, f3)) + jnp.concatenate(prior, axis=1))
    step = 64
    for row, kern_ref in ((0, own_ref), (1, other_ref)):
        for i in range(0, half, step):
            total = jnp.zeros((step, LANES), F32)
            for g in range(count // LANES):
                at = slice(g * LANES, (g + 1) * LANES)
                kern = kern_ref[i : i + step, at]
                total = total + kern * kern * finv_ref[:, at]
            acc[i : i + step] = total
        t_ref[row : row + 1] = jnp.sum(acc[...].T, axis=0, keepdims=True)


def weights(kern, finv, tinv, rinv):
    weight = kern * kern * (kern * finv * tinv - rinv)
    high = weight.astype(BF16)
    return high, (weight - high.astype(F32)).astype(BF16)


def grad_body(own_ref, other_ref, rinv_ref, finv_ref, t0, t1, t2, t3, z_ref, zo_ref, c_ref, *outs):
    pieces_x, pieces_h, embeds = outs[:SIDE], outs[SIDE : 2 * SIDE], outs[2 * SIDE : -4]
    zt, ts, rs, acc = outs[-4:]
    half, count = own_ref.shape
    inner = count // (SIDE * SIDE)
    tinv = 1.0 / four((t0, t1, t2, t3))
    points = (z_ref[...].astype(F32), zo_ref[...])
    kerns = (own_ref, other_ref)
    for p in range(CORES):
        ts[p] = spread(tinv[p : p + 1])
        rs[p] = spread(rinv_ref[p : p + 1])
        zt[p, :LANES] = (-SCALE * points[p].T).astype(BF16)
        zt[p, LANES:] = jnp.full((ONES, half), SCALE, BF16)
    acc[...] = jnp.zeros_like(acc)
    core = lax.axis_index("pts") % CORES
    place = lax.axis_index("pts") // CORES
    x, h = place // SIDE, place % SIDE
    for s in (2, 1, 3, 0):
        for t in range(SIDE):
            block = (x ^ s) * SIDE + (h ^ t)
            at = pl.ds(pl.multiple_of(block * inner, inner), inner)
            c = c_ref[block_rows(block, inner, core), :]
            wide = jnp.concatenate([c, jnp.ones((inner, LANES), BF16)], axis=1)
            sums = jnp.zeros((LANES + ONES, inner), F32)
            for p in range(CORES):
                high, low = weights(
                    kerns[p][:, at],
                    finv_ref[:, at],
                    tile_lanes(ts[p], inner),
                    tile_lanes(rs[p], inner),
                )
                sums += jnp.dot(zt[p], high, preferred_element_type=F32)
                sums += jnp.dot(zt[p], low, preferred_element_type=F32)
                acc[p] += jnp.dot(high, wide, preferred_element_type=F32) + jnp.dot(
                    low, wide, preferred_element_type=F32
                )
            grad = sums[:LANES] + sums[LANES : LANES + 1] * c.astype(F32).T
            pieces_x[s][:, t * inner : (t + 1) * inner] = grad[:ROWS_X]
            pieces_h[t][:, s * inner : (s + 1) * inner] = grad[ROWS_X:]
    for p in range(CORES):
        sums = acc[p]
        embeds[p][...] = SCALE * (sums[:, LANES:] * points[p] - sums[:, :LANES])


def split_body(*refs):
    ins, outs = refs[:SIDE], refs[SIDE:]
    inner = outs[0].shape[1]
    for t in range(SIDE):
        outs[t][...] = four([r.at[:, t * inner : (t + 1) * inner] for r in ins])


def final_body(*refs):
    ins, out = refs[:-1], refs[-1]
    out[...] = jnp.concatenate([four(ins[:SIDE]), four(ins[SIDE:])], axis=0).T


def embed_split_body(mine, theirs, *outs):
    y = lax.axis_index("ctr") % SIDE
    rows = outs[0].shape[0]
    for s in range(SIDE):
        at = pl.ds(pl.multiple_of((y ^ s) * rows, rows), rows)
        outs[s][...] = mine[at, :] + theirs[at, :]


def embed_join_body(*refs):
    ins, out = refs[:-1], refs[-1]
    y = lax.axis_index("ctr") % SIDE
    rows = ins[0].shape[0]
    for s in range(SIDE):
        out[pl.ds(pl.multiple_of((y ^ s) * rows, rows), rows), :] = ins[s][...]


VMEM = pl.BlockSpec(memory_space=pltpu.VMEM)


def call(body, outs, *args, scratch=(), limit=2, name=None, flops=0):
    shapes = tuple(jax.ShapeDtypeStruct(shape, F32) for shape in outs)
    moved = sum(a.size * a.dtype.itemsize for a in args)
    out = pl.pallas_call(
        body,
        out_shape=shapes,
        in_specs=[VMEM] * len(args),
        out_specs=tuple(VMEM for _ in outs),
        scratch_shapes=scratch,
        compiler_params=pltpu.CompilerParams(vmem_limit_bytes=limit * MIB),
        cost_estimate=pl.CostEstimate(flops=flops, bytes_accessed=moved, transcendentals=0),
        name=name,
    )(*args)
    return out if len(out) > 1 else out[0]


def body(embeddings, centres, prior_freq):
    n_pts, n_ctr = lax.axis_size("pts"), lax.axis_size("ctr")
    half, width = embeddings.shape
    inner = centres.shape[0] // n_pts
    count = centres.shape[0] // CORES
    prior = prior_freq.reshape(1, centres.shape[0])

    def swap_core(v):
        return lax.ppermute(v, "pts", core_perm(n_pts))

    def swap_zl(v):
        return lax.ppermute(v, "ctr", ctr_perm(n_ctr, SIDE))

    def around_y(vs):
        return [vs[0]] + [lax.ppermute(vs[s], "ctr", ctr_perm(n_ctr, s)) for s in (1, 2, 3)]

    def around_x(vs):
        return [vs[0]] + [lax.ppermute(vs[s], "pts", x_perm(n_pts, s)) for s in (1, 2, 3)]

    def around_h(vs):
        return [vs[0]] + [lax.ppermute(vs[s], "pts", h_perm(n_pts, s)) for s in (1, 2, 3)]

    def over_ctr(v):
        v = call(swap_add_body, [v.shape], v, swap_core(v), name="sum_core")
        v = call(add_body, [v.shape], v, swap_zl(v), name="sum_zl")
        return around_y([v] * SIDE)

    rows = (CORES, half)
    z_other = swap_core(embeddings.astype(F32))
    kern_scratch = [pltpu.VMEM((half, width), BF16), pltpu.VMEM((half, LANES), F32)]
    kern_own, row = call(
        own_body,
        [(half, count), (1, half)],
        embeddings,
        centres,
        scratch=kern_scratch,
        limit=20,
        name="kern_own",
    )
    kern_other, row = call(
        other_body,
        [(half, count), rows],
        z_other,
        centres,
        row,
        scratch=kern_scratch,
        limit=20,
        name="kern_other",
    )
    freq, rinv = call(
        freq_body, [(1, count), rows], kern_own, kern_other, *over_ctr(row), limit=20, name="freq"
    )
    freq = call(add_body, [freq.shape], *around_x([freq] * SIDE), name="sum_x")
    target, finv = call(
        target_body,
        [rows, (1, count)],
        kern_own,
        kern_other,
        *around_h([freq] * SIDE),
        prior,
        scratch=[pltpu.VMEM((half, LANES), F32)],
        limit=20,
        name="target",
    )
    *pieces, mine, other = call(
        grad_body,
        [(ROWS_X, SIDE * inner)] * SIDE
        + [(width - ROWS_X, SIDE * inner)] * SIDE
        + [(half, width)] * 2,
        kern_own,
        kern_other,
        rinv,
        finv,
        *over_ctr(target),
        embeddings,
        z_other,
        centres,
        scratch=[
            pltpu.VMEM((CORES, width + ONES, half), BF16),
            pltpu.VMEM((CORES, half, LANES), F32),
            pltpu.VMEM((CORES, half, LANES), F32),
            pltpu.VMEM((CORES, half, 2 * LANES), F32),
        ],
        limit=24,
        name="grad",
    )
    by_x, by_h = around_x(pieces[:SIDE]), around_h(pieces[SIDE:])

    quarter = (half // SIDE, width)
    embed = call(embed_split_body, [quarter] * SIDE, mine, swap_core(other), name="embed_split")
    embed = call(add_body, [quarter], *around_y(embed), name="embed_y")
    embed = call(add_body, [quarter], embed, swap_zl(embed), name="embed_zl")
    embed = call(embed_join_body, [(half, width)], *around_y([embed] * SIDE), name="embed_join")

    by_x = call(split_body, [(ROWS_X, inner)] * SIDE, *by_x, name="split_x")
    by_h = call(split_body, [(width - ROWS_X, inner)] * SIDE, *by_h, name="split_h")
    grad = call(
        final_body, [(inner, width)], *around_h(by_x), *around_x(by_h), name="final"
    )
    return embed, grad.reshape(1, inner, width)


def solution(mesh):
    in_specs = (P("pts", None), P("ctr", None), P("ctr"))
    out_specs = (P("pts", None), P("ctr", "pts", None))
    return jax.shard_map(body, mesh=mesh, in_specs=in_specs, out_specs=out_specs, check_vma=False)
```

time: 135 us -> 120 us (0.89)
  waiting for transfers between devices: 48.2 us -> 36.7 us
  starting transfers between devices: 51 us -> 59.4 us
  local copies, waits for them, and re-layouts: 10.7 us -> 4.09 us
  Pallas kernels: 20.9 us -> 17.6 us
  other arithmetic: 3.42 us -> 0.93 us
    ppermute x29 -> x33, waiting for transfers between devices: 42.8 us -> 34.7 us  [the longest x9 13.5 us: around_h(): lax.ppermute(vs[s], 'pts', h_perm(n_pts, s))]
    ppermute x29 -> x33, starting transfers between devices: 50.7 us -> 58.6 us  [the longest x9 23.3 us: around_h(): lax.ppermute(vs[s], 'pts', h_perm(n_pts, s))]
    unnamed x28 -> x12, local copies, waits for them, and re-layouts: 8.49 us -> 4.09 us
    ppermute x4, waiting for transfers between devices: 5.37 us -> 1.98 us  [swap_core(): return lax.ppermute(v, 'pts', core_perm(n_pts))]
    pallas_call x8 -> x17, Pallas kernels: 20.9 us -> 17.6 us  [call(): pl.pallas_call(body, out_shape=shapes, in_specs=[VMEM] * len(args), out_s...]
    add x9 -> x0, other arithmetic: 1.64 us -> none  [the longest x3 0.79 us: body(): embed = embed + lax.ppermute(embed, 'ctr', ctr_perm(n_ctr, s))]
    reshape x1 -> x0, local copies, waits for them, and re-layouts: 1.39 us -> none  [body(): prior_freq.reshape(n_pts // CORES, CORES, inner)]
  transfers between devices with their start and end apart: 33 -> 37, of which waited for: 17 -> 19; matrix products, arithmetic and copies ran while one was open for 2% -> 0% of each run, Pallas kernels for 1% -> 3%
where the time goes in v2:
time: 120 us
  starting transfers between devices  59.4 us (50%)
  waiting for transfers between devices  36.7 us (31%)
  Pallas kernels  17.6 us (15%)
  local copies, waits for them, and re-layouts  4.09 us (3%)
    ppermute x9, starting transfers between devices, around_h(): lax.ppermute(vs[s], 'pts', h_perm(n_pts, s))  23.3 us
    ppermute x12, starting transfers between devices, around_y(): lax.ppermute(vs[s], 'ctr', ctr_perm(n_ctr, s))  17.8 us
    pallas_call x17, Pallas kernels, call(): pl.pallas_call(body, out_shape=shapes, in_specs=[VMEM] * len(args), out_s...  17.6 us
    ppermute x9, starting transfers between devices, around_x(): lax.ppermute(vs[s], 'pts', x_perm(n_pts, s))  13.7 us
    ppermute x9, waiting for transfers between devices, around_h(): lax.ppermute(vs[s], 'pts', h_perm(n_pts, s))  13.5 us
    ppermute x12, waiting for transfers between devices, around_y(): lax.ppermute(vs[s], 'ctr', ctr_perm(n_ctr, s))  12.2 us
    ppermute x9, waiting for transfers between devices, around_x(): lax.ppermute(vs[s], 'pts', x_perm(n_pts, s))  4.72 us
    ppermute x3, waiting for transfers between devices, swap_zl(): return lax.ppermute(v, 'ctr', ctr_perm(n_ctr, SIDE))  4.35 us
  transfers between devices with their start and end apart: 37, of which 19 were waited for; matrix products, arithmetic and copies ran while one was open for 0% of the time, Pallas kernels for 3%

profile of v2, /device:TPU:32, one launch (start us, length us, event | category | flops | bytes accessed | tf_op | source)
XLA Modules:
  0.0 119.5 jit_solution(745663178684479182)
XLA Ops:
  4.2 2.2 %kern_own.1 = (f32[512,4096]{1,0:T(8,128)S(1)}, f32[1,512]{1,0:T(1,128)S(1)}) custom-call(bf16[512,128]{1,0:T(8,128)(2,1)S(1)} %copy-done.3, bf16[8192,128]{1,0:T(8,128)(2,1)S(1)} %copy-done), custom_call_target="tpu_custom_call" | custom-call | bytes 2228224 | tf_op jit(solution)/shard_map/kern_own/pallas_call | solution.py:205
  7.9 2.1 %kern_other.1 = (f32[512,4096]{1,0:T(8,128)S(1)}, f32[2,512]{1,0:T(2,128)S(1)}) custom-call(f32[512,128]{1,0:T(8,128)S(1)} %collective-permute-done.zo_ref, bf16[8192,128]{1,0:T(8,128)(2,1)S(1)} %copy-done.1, f32[1,512]{1,0:T(1,128)S(1)} %get-tuple-element.33.row_ref), custom_call_target="tpu_custom_call" | custom-call | bytes 2361344 | tf_op jit(solution)/shard_map/kern_other/pallas_call | solution.py:205
  11.5 1.8 %collective-permute-start.2 = (f32[2,512]{1,0:T(2,128)S(1)}, f32[2,512]{1,0:T(2,128)S(1)}, u32[]{:S(2)}, u32[]{:S(2)}) collective-permute-start(f32[2,512]{1,0:T(2,128)S(1)} %sum_core.2.refs_0_), channel_id=1, source_target_pairs={{0,4},{1,5},{2,6},{3,7},{4,0},{5,1},{6,2},{7,3},{8,12},{9,13},{10,... | collective-permute-start | bytes 12296 | tf_op jit(solution)/shard_map/ppermute | solution.py:229
  15.1 3.0 %collective-permute-start.5 = (f32[2,512]{1,0:T(2,128)S(1)}, f32[2,512]{1,0:T(2,128)S(1)}, u32[]{:S(2)}, u32[]{:S(2)}) collective-permute-start(f32[2,512]{1,0:T(2,128)S(1)} %sum_zl.2.r0), channel_id=1, source_target_pairs={{0,3},{1,2},{2,1},{3,0},{4,7},{5,6},{6,5},{7,4},{8,11},{9,10},{10,... | collective-permute-start | bytes 12296 | tf_op jit(solution)/shard_map/ppermute | solution.py:232
  19.9 3.3 %collective-permute-done.4.r2 = f32[2,512]{1,0:T(2,128)S(1)} collective-permute-done((f32[2,512]{1,0:T(2,128)S(1)}, f32[2,512]{1,0:T(2,128)S(1)}, u32[]{:S(2)}, u32[]{:S(2)}) %collective-permute-start.4) | collective-permute-done | bytes 4128 | tf_op jit(solution)/shard_map/ppermute | solution.py:232
  24.9 2.8 %collective-permute-start.8 = (f32[1,4096]{1,0:T(1,128)S(1)}, f32[1,4096]{1,0:T(1,128)S(1)}, u32[]{:S(2)}, u32[]{:S(2)}) collective-permute-start(f32[1,4096]{1,0:T(1,128)S(1)} %get-tuple-element.37.refs_0_), channel_id=1, source_target_pairs={{0,192},{8,200},{16,208},{24,216},{32,224},{40,232},{48,240},{56,2... | collective-permute-start | bytes 49160 | tf_op jit(solution)/shard_map/ppermute | solution.py:235
  29.9 3.1 %collective-permute-done.7.refs_2_ = f32[1,4096]{1,0:T(1,128)S(1)} collective-permute-done((f32[1,4096]{1,0:T(1,128)S(1)}, f32[1,4096]{1,0:T(1,128)S(1)}, u32[]{:S(2)}, u32[]{:S(2)}) %collective-permute-start.7) | collective-permute-done | bytes 16416 | tf_op jit(solution)/shard_map/ppermute | solution.py:235
  33.0 5.5 %collective-permute-start.11 = (f32[1,4096]{1,0:T(1,128)S(1)}, f32[1,4096]{1,0:T(1,128)S(1)}, u32[]{:S(2)}, u32[]{:S(2)}) collective-permute-start(f32[1,4096]{1,0:T(1,128)S(1)} %sum_x.1.f0), channel_id=1, source_target_pairs={{0,48},{8,56},{16,32},{24,40},{32,16},{40,24},{48,0},{56,8},{64,11... | collective-permute-start | bytes 49160 | tf_op jit(solution)/shard_map/ppermute | solution.py:238
  41.0 5.2 %collective-permute-done.10.f2 = f32[1,4096]{1,0:T(1,128)S(1)} collective-permute-done((f32[1,4096]{1,0:T(1,128)S(1)}, f32[1,4096]{1,0:T(1,128)S(1)}, u32[]{:S(2)}, u32[]{:S(2)}) %collective-permute-start.10) | collective-permute-done | bytes 16416 | tf_op jit(solution)/shard_map/ppermute | solution.py:238
  50.2 2.6 %collective-permute-done.13.refs_1_ = f32[2,512]{1,0:T(2,128)S(1)} collective-permute-done((f32[2,512]{1,0:T(2,128)S(1)}, f32[2,512]{1,0:T(2,128)S(1)}, u32[]{:S(2)}, u32[]{:S(2)}) %collective-permute-start.13) | collective-permute-done | bytes 4128 | tf_op jit(solution)/shard_map/ppermute | solution.py:229
  55.0 1.9 %collective-permute-start.14 = (f32[2,512]{1,0:T(2,128)S(1)}, f32[2,512]{1,0:T(2,128)S(1)}, u32[]{:S(2)}, u32[]{:S(2)}) collective-permute-start(f32[2,512]{1,0:T(2,128)S(1)} %sum_zl.3.t0), channel_id=1, source_target_pairs={{0,1},{1,0},{2,3},{3,2},{4,5},{5,4},{6,7},{7,6},{8,9},{9,8},{10,11... | collective-permute-start | bytes 12296 | tf_op jit(solution)/shard_map/ppermute | solution.py:232
  59.2 8.1 %grad.1 = (f32[88,1024]{1,0:T(8,128)S(1)}, f32[88,1024]{1,0:T(8,128)S(1)}, f32[88,1024]{1,0:T(8,128)S(1)}, f32[88,1024]{1,0:T(8,128)S(1)}, f32[40,1024]{1,0:T(8,...) custom-call(f32[512,4096]{1,0:T(8,128)S(1)} %get-tuple-element.32.ow, ...), custom_call_target="tpu_custom_call" | custom-call | bytes 19304448 | tf_op jit(solution)/shard_map/grad/pallas_call | solution.py:205
  67.7 2.6 %collective-permute-start.26 = (f32[88,1024]{1,0:T(8,128)S(1)}, f32[88,1024]{1,0:T(8,128)S(1)}, u32[]{:S(2)}, u32[]{:S(2)}) collective-permute-start(f32[88,1024]{1,0:T(8,128)S(1)} %get-tuple-element.48), channel_id=1, source_target_pairs={{0,128},{8,136},{16,144},{24,152},{32,160},{40,168},{48,176},{56,1... | collective-permute-start | bytes 1081352 | tf_op jit(solution)/shard_map/ppermute | solution.py:235
  70.3 1.9 %collective-permute-start.27 = (f32[88,1024]{1,0:T(8,128)S(1)}, f32[88,1024]{1,0:T(8,128)S(1)}, u32[]{:S(2)}, u32[]{:S(2)}) collective-permute-start(f32[88,1024]{1,0:T(8,128)S(1)} %get-tuple-element.49), channel_id=1, source_target_pairs={{0,192},{8,200},{16,208},{24,216},{32,224},{40,232},{48,240},{56,2... | collective-permute-start | bytes 1081352 | tf_op jit(solution)/shard_map/ppermute | solution.py:235
  73.6 2.1 %collective-permute-start.19 = (f32[128,128]{1,0:T(8,128)S(1)}, f32[128,128]{1,0:T(8,128)S(1)}, u32[]{:S(2)}, u32[]{:S(2)}) collective-permute-start(f32[128,128]{1,0:T(8,128)S(1)} %get-tuple-element.44), channel_id=1, source_target_pairs={{0,2},{1,3},{2,0},{3,1},{4,6},{5,7},{6,4},{7,5},{8,10},{9,11},{10,... | collective-permute-start | bytes 196616 | tf_op jit(solution)/shard_map/ppermute | solution.py:232
  77.0 1.9 %collective-permute-start.20 = (f32[128,128]{1,0:T(8,128)S(1)}, f32[128,128]{1,0:T(8,128)S(1)}, u32[]{:S(2)}, u32[]{:S(2)}) collective-permute-start(f32[128,128]{1,0:T(8,128)S(1)} %get-tuple-element.45), channel_id=1, source_target_pairs={{0,3},{1,2},{2,1},{3,0},{4,7},{5,6},{6,5},{7,4},{8,11},{9,10},{10,... | collective-permute-start | bytes 196616 | tf_op jit(solution)/shard_map/ppermute | solution.py:232
  82.5 2.9 %collective-permute-start.32 = (f32[40,1024]{1,0:T(8,128)S(1)}, f32[40,1024]{1,0:T(8,128)S(1)}, u32[]{:S(2)}, u32[]{:S(2)}) collective-permute-start(f32[40,1024]{1,0:T(8,128)S(1)} %get-tuple-element.56), channel_id=1, source_target_pairs={{0,32},{8,40},{16,48},{24,56},{32,0},{40,8},{48,16},{56,24},{64,96... | collective-permute-start | bytes 491528 | tf_op jit(solution)/shard_map/ppermute | solution.py:238
  85.4 2.3 %collective-permute-start.33 = (f32[40,1024]{1,0:T(8,128)S(1)}, f32[40,1024]{1,0:T(8,128)S(1)}, u32[]{:S(2)}, u32[]{:S(2)}) collective-permute-start(f32[40,1024]{1,0:T(8,128)S(1)} %get-tuple-element.57), channel_id=1, source_target_pairs={{0,48},{8,56},{16,32},{24,40},{32,16},{40,24},{48,0},{56,8},{64,11... | collective-permute-start | bytes 491528 | tf_op jit(solution)/shard_map/ppermute | solution.py:238
  91.3 3.1 %collective-permute-done.31.refs_1_ = f32[40,1024]{1,0:T(8,128)S(1)} collective-permute-done((f32[40,1024]{1,0:T(8,128)S(1)}, f32[40,1024]{1,0:T(8,128)S(1)}, u32[]{:S(2)}, u32[]{:S(2)}) %collective-permute-start.31) | collective-permute-done | bytes 163872 | tf_op jit(solution)/shard_map/ppermute | solution.py:238
  94.4 5.2 %collective-permute-done.32.refs_2_ = f32[40,1024]{1,0:T(8,128)S(1)} collective-permute-done((f32[40,1024]{1,0:T(8,128)S(1)}, f32[40,1024]{1,0:T(8,128)S(1)}, u32[]{:S(2)}, u32[]{:S(2)}) %collective-permute-start.32) | collective-permute-done | bytes 163872 | tf_op jit(solution)/shard_map/ppermute | solution.py:238
  99.7 3.4 %collective-permute-start.35 = (f32[40,256]{1,0:T(8,128)S(1)}, f32[40,256]{1,0:T(8,128)S(1)}, u32[]{:S(2)}, u32[]{:S(2)}) collective-permute-start(f32[40,256]{1,0:T(8,128)S(1)} %get-tuple-element.60), channel_id=1, source_target_pairs={{0,128},{8,136},{16,144},{24,152},{32,160},{40,168},{48,176},{56,1... | collective-permute-start | bytes 122888 | tf_op jit(solution)/shard_map/ppermute | solution.py:235
  104.4 3.1 %collective-permute-start.29 = (f32[88,256]{1,0:T(8,128)S(1)}, f32[88,256]{1,0:T(8,128)S(1)}, u32[]{:S(2)}, u32[]{:S(2)}) collective-permute-start(f32[88,256]{1,0:T(8,128)S(1)} %get-tuple-element.52), channel_id=1, source_target_pairs={{0,32},{8,40},{16,48},{24,56},{32,0},{40,8},{48,16},{56,24},{64,96... | collective-permute-start | bytes 270344 | tf_op jit(solution)/shard_map/ppermute | solution.py:238
  107.5 3.7 %collective-permute-start.30 = (f32[88,256]{1,0:T(8,128)S(1)}, f32[88,256]{1,0:T(8,128)S(1)}, u32[]{:S(2)}, u32[]{:S(2)}) collective-permute-start(f32[88,256]{1,0:T(8,128)S(1)} %get-tuple-element.53), channel_id=1, source_target_pairs={{0,48},{8,56},{16,32},{24,40},{32,16},{40,24},{48,0},{56,8},{64,11... | collective-permute-start | bytes 270344 | tf_op jit(solution)/shard_map/ppermute | solution.py:238
  116.8 2.0 %collective-permute-done.23.refs_2_ = f32[128,128]{1,0:T(8,128)S(1)} collective-permute-done((f32[128,128]{1,0:T(8,128)S(1)}, f32[128,128]{1,0:T(8,128)S(1)}, u32[]{:S(2)}, u32[]{:S(2)}) %collective-permute-start.23) | collective-permute-done | bytes 65568 | tf_op jit(solution)/shard_map/ppermute | solution.py:232
  (80 shorter events, 43.0 us)
Async XLA Ops:
  18.1 5.1 %collective-permute-start.4 = (f32[2,512]{1,0:T(2,128)S(1)}, f32[2,512]{1,0:T(2,128)S(1)}, u32[]{:S(2)}, u32[]{:S(2)}) collective-permute-start(f32[2,512]{1,0:T(2,128)S(1)} %sum_zl.2.r0), channel_id=1, source_target_pairs={{0,2},{1,3},{2,0},{3,1},{4,6},{5,7},{6,4},{7,5},{8,10},{9,11},{10,... | collective-permute-start | bytes 12296 | tf_op jit(solution)/shard_map/ppermute | solution.py:232
  24.9 5.0 %collective-permute-start.8 = (f32[1,4096]{1,0:T(1,128)S(1)}, f32[1,4096]{1,0:T(1,128)S(1)}, u32[]{:S(2)}, u32[]{:S(2)}) collective-permute-start(f32[1,4096]{1,0:T(1,128)S(1)} %get-tuple-element.37.refs_0_), channel_id=1, source_target_pairs={{0,192},{8,200},{16,208},{24,216},{32,224},{40,232},{48,240},{56,2... | collective-permute-start | bytes 49160 | tf_op jit(solution)/shard_map/ppermute | solution.py:235
  27.7 5.2 %collective-permute-start.7 = (f32[1,4096]{1,0:T(1,128)S(1)}, f32[1,4096]{1,0:T(1,128)S(1)}, u32[]{:S(2)}, u32[]{:S(2)}) collective-permute-start(f32[1,4096]{1,0:T(1,128)S(1)} %get-tuple-element.37.refs_0_), channel_id=1, source_target_pairs={{0,128},{8,136},{16,144},{24,152},{32,160},{40,168},{48,176},{56,1... | collective-permute-start | bytes 49160 | tf_op jit(solution)/shard_map/ppermute | solution.py:235
  33.0 7.9 %collective-permute-start.11 = (f32[1,4096]{1,0:T(1,128)S(1)}, f32[1,4096]{1,0:T(1,128)S(1)}, u32[]{:S(2)}, u32[]{:S(2)}) collective-permute-start(f32[1,4096]{1,0:T(1,128)S(1)} %sum_x.1.f0), channel_id=1, source_target_pairs={{0,48},{8,56},{16,32},{24,40},{32,16},{40,24},{48,0},{56,8},{64,11... | collective-permute-start | bytes 49160 | tf_op jit(solution)/shard_map/ppermute | solution.py:238
  38.5 7.6 %collective-permute-start.10 = (f32[1,4096]{1,0:T(1,128)S(1)}, f32[1,4096]{1,0:T(1,128)S(1)}, u32[]{:S(2)}, u32[]{:S(2)}) collective-permute-start(f32[1,4096]{1,0:T(1,128)S(1)} %sum_x.1.f0), channel_id=1, source_target_pairs={{0,32},{8,40},{16,48},{24,56},{32,0},{40,8},{48,16},{56,24},{64,96... | collective-permute-start | bytes 49160 | tf_op jit(solution)/shard_map/ppermute | solution.py:238
  39.9 6.2 %collective-permute-start.9 = (f32[1,4096]{1,0:T(1,128)S(1)}, f32[1,4096]{1,0:T(1,128)S(1)}, u32[]{:S(2)}, u32[]{:S(2)}) collective-permute-start(f32[1,4096]{1,0:T(1,128)S(1)} %sum_x.1.f0), channel_id=1, source_target_pairs={{0,16},{8,24},{16,0},{24,8},{32,48},{40,56},{48,32},{56,40},{64,80... | collective-permute-start | bytes 49160 | tf_op jit(solution)/shard_map/ppermute | solution.py:238
  54.1 5.1 %collective-permute-start.15 = (f32[2,512]{1,0:T(2,128)S(1)}, f32[2,512]{1,0:T(2,128)S(1)}, u32[]{:S(2)}, u32[]{:S(2)}) collective-permute-start(f32[2,512]{1,0:T(2,128)S(1)} %sum_zl.3.t0), channel_id=1, source_target_pairs={{0,2},{1,3},{2,0},{3,1},{4,6},{5,7},{6,4},{7,5},{8,10},{9,11},{10,... | collective-permute-start | bytes 12296 | tf_op jit(solution)/shard_map/ppermute | solution.py:232
  67.4 18.0 %collective-permute-start.25 = (f32[88,1024]{1,0:T(8,128)S(1)}, f32[88,1024]{1,0:T(8,128)S(1)}, u32[]{:S(2)}, u32[]{:S(2)}) collective-permute-start(f32[88,1024]{1,0:T(8,128)S(1)} %get-tuple-element.47), channel_id=1, source_target_pairs={{0,64},{8,72},{16,80},{24,88},{32,96},{40,104},{48,112},{56,120},{... | collective-permute-start | bytes 1081352 | tf_op jit(solution)/shard_map/ppermute | solution.py:235
  67.7 20.0 %collective-permute-start.26 = (f32[88,1024]{1,0:T(8,128)S(1)}, f32[88,1024]{1,0:T(8,128)S(1)}, u32[]{:S(2)}, u32[]{:S(2)}) collective-permute-start(f32[88,1024]{1,0:T(8,128)S(1)} %get-tuple-element.48), channel_id=1, source_target_pairs={{0,128},{8,136},{16,144},{24,152},{32,160},{40,168},{48,176},{56,1... | collective-permute-start | bytes 1081352 | tf_op jit(solution)/shard_map/ppermute | solution.py:235
  70.3 19.1 %collective-permute-start.27 = (f32[88,1024]{1,0:T(8,128)S(1)}, f32[88,1024]{1,0:T(8,128)S(1)}, u32[]{:S(2)}, u32[]{:S(2)}) collective-permute-start(f32[88,1024]{1,0:T(8,128)S(1)} %get-tuple-element.49), channel_id=1, source_target_pairs={{0,192},{8,200},{16,208},{24,216},{32,224},{40,232},{48,240},{56,2... | collective-permute-start | bytes 1081352 | tf_op jit(solution)/shard_map/ppermute | solution.py:235
  73.6 5.8 %collective-permute-start.19 = (f32[128,128]{1,0:T(8,128)S(1)}, f32[128,128]{1,0:T(8,128)S(1)}, u32[]{:S(2)}, u32[]{:S(2)}) collective-permute-start(f32[128,128]{1,0:T(8,128)S(1)} %get-tuple-element.44), channel_id=1, source_target_pairs={{0,2},{1,3},{2,0},{3,1},{4,6},{5,7},{6,4},{7,5},{8,10},{9,11},{10,... | collective-permute-start | bytes 196616 | tf_op jit(solution)/shard_map/ppermute | solution.py:232
  77.0 5.5 %collective-permute-start.20 = (f32[128,128]{1,0:T(8,128)S(1)}, f32[128,128]{1,0:T(8,128)S(1)}, u32[]{:S(2)}, u32[]{:S(2)}) collective-permute-start(f32[128,128]{1,0:T(8,128)S(1)} %get-tuple-element.45), channel_id=1, source_target_pairs={{0,3},{1,2},{2,1},{3,0},{4,7},{5,6},{6,5},{7,4},{8,11},{9,10},{10,... | collective-permute-start | bytes 196616 | tf_op jit(solution)/shard_map/ppermute | solution.py:232
  79.4 15.0 %collective-permute-start.31 = (f32[40,1024]{1,0:T(8,128)S(1)}, f32[40,1024]{1,0:T(8,128)S(1)}, u32[]{:S(2)}, u32[]{:S(2)}) collective-permute-start(f32[40,1024]{1,0:T(8,128)S(1)} %get-tuple-element.55), channel_id=1, source_target_pairs={{0,16},{8,24},{16,0},{24,8},{32,48},{40,56},{48,32},{56,40},{64,80... | collective-permute-start | bytes 491528 | tf_op jit(solution)/shard_map/ppermute | solution.py:238
  82.5 17.0 %collective-permute-start.32 = (f32[40,1024]{1,0:T(8,128)S(1)}, f32[40,1024]{1,0:T(8,128)S(1)}, u32[]{:S(2)}, u32[]{:S(2)}) collective-permute-start(f32[40,1024]{1,0:T(8,128)S(1)} %get-tuple-element.56), channel_id=1, source_target_pairs={{0,32},{8,40},{16,48},{24,56},{32,0},{40,8},{48,16},{56,24},{64,96... | collective-permute-start | bytes 491528 | tf_op jit(solution)/shard_map/ppermute | solution.py:238
  85.4 14.1 %collective-permute-start.33 = (f32[40,1024]{1,0:T(8,128)S(1)}, f32[40,1024]{1,0:T(8,128)S(1)}, u32[]{:S(2)}, u32[]{:S(2)}) collective-permute-start(f32[40,1024]{1,0:T(8,128)S(1)} %get-tuple-element.57), channel_id=1, source_target_pairs={{0,48},{8,56},{16,32},{24,40},{32,16},{40,24},{48,0},{56,8},{64,11... | collective-permute-start | bytes 491528 | tf_op jit(solution)/shard_map/ppermute | solution.py:238
  87.7 19.7 %collective-permute-start.21 = (f32[128,128]{1,0:T(8,128)S(1)}, f32[128,128]{1,0:T(8,128)S(1)}, u32[]{:S(2)}, u32[]{:S(2)}) collective-permute-start(f32[128,128]{1,0:T(8,128)S(1)} %embed_y.1.refs_0_), channel_id=1, source_target_pairs={{0,4},{1,5},{2,6},{3,7},{4,0},{5,1},{6,2},{7,3},{8,12},{9,13},{10,... | collective-permute-start | bytes 196616 | tf_op jit(solution)/shard_map/ppermute | solution.py:229
  89.6 24.3 %collective-permute-start.28 = (f32[88,256]{1,0:T(8,128)S(1)}, f32[88,256]{1,0:T(8,128)S(1)}, u32[]{:S(2)}, u32[]{:S(2)}) collective-permute-start(f32[88,256]{1,0:T(8,128)S(1)} %get-tuple-element.51), channel_id=1, source_target_pairs={{0,16},{8,24},{16,0},{24,8},{32,48},{40,56},{48,32},{56,40},{64,80... | collective-permute-start | bytes 270344 | tf_op jit(solution)/shard_map/ppermute | solution.py:238
  99.7 11.5 %collective-permute-start.35 = (f32[40,256]{1,0:T(8,128)S(1)}, f32[40,256]{1,0:T(8,128)S(1)}, u32[]{:S(2)}, u32[]{:S(2)}) collective-permute-start(f32[40,256]{1,0:T(8,128)S(1)} %get-tuple-element.60), channel_id=1, source_target_pairs={{0,128},{8,136},{16,144},{24,152},{32,160},{40,168},{48,176},{56,1... | collective-permute-start | bytes 122888 | tf_op jit(solution)/shard_map/ppermute | solution.py:235
  103.1 10.0 %collective-permute-start.36 = (f32[40,256]{1,0:T(8,128)S(1)}, f32[40,256]{1,0:T(8,128)S(1)}, u32[]{:S(2)}, u32[]{:S(2)}) collective-permute-start(f32[40,256]{1,0:T(8,128)S(1)} %get-tuple-element.61), channel_id=1, source_target_pairs={{0,192},{8,200},{16,208},{24,216},{32,224},{40,232},{48,240},{56,2... | collective-permute-start | bytes 122888 | tf_op jit(solution)/shard_map/ppermute | solution.py:235
  104.4 11.0 %collective-permute-start.29 = (f32[88,256]{1,0:T(8,128)S(1)}, f32[88,256]{1,0:T(8,128)S(1)}, u32[]{:S(2)}, u32[]{:S(2)}) collective-permute-start(f32[88,256]{1,0:T(8,128)S(1)} %get-tuple-element.52), channel_id=1, source_target_pairs={{0,32},{8,40},{16,48},{24,56},{32,0},{40,8},{48,16},{56,24},{64,96... | collective-permute-start | bytes 270344 | tf_op jit(solution)/shard_map/ppermute | solution.py:238
  107.5 7.9 %collective-permute-start.30 = (f32[88,256]{1,0:T(8,128)S(1)}, f32[88,256]{1,0:T(8,128)S(1)}, u32[]{:S(2)}, u32[]{:S(2)}) collective-permute-start(f32[88,256]{1,0:T(8,128)S(1)} %get-tuple-element.53), channel_id=1, source_target_pairs={{0,48},{8,56},{16,32},{24,40},{32,16},{40,24},{48,0},{56,8},{64,11... | collective-permute-start | bytes 270344 | tf_op jit(solution)/shard_map/ppermute | solution.py:238
  111.2 5.6 %collective-permute-start.24 = (f32[128,128]{1,0:T(8,128)S(1)}, f32[128,128]{1,0:T(8,128)S(1)}, u32[]{:S(2)}, u32[]{:S(2)}) collective-permute-start(f32[128,128]{1,0:T(8,128)S(1)} %embed_zl.1.refs_0_), channel_id=1, source_target_pairs={{0,3},{1,2},{2,1},{3,0},{4,7},{5,6},{6,5},{7,4},{8,11},{9,10},{10,... | collective-permute-start | bytes 196616 | tf_op jit(solution)/shard_map/ppermute | solution.py:232
  113.0 5.8 %collective-permute-start.23 = (f32[128,128]{1,0:T(8,128)S(1)}, f32[128,128]{1,0:T(8,128)S(1)}, u32[]{:S(2)}, u32[]{:S(2)}) collective-permute-start(f32[128,128]{1,0:T(8,128)S(1)} %embed_zl.1.refs_0_), channel_id=1, source_target_pairs={{0,2},{1,3},{2,0},{3,1},{4,6},{5,7},{6,4},{7,5},{8,10},{9,11},{10,... | collective-permute-start | bytes 196616 | tf_op jit(solution)/shard_map/ppermute | solution.py:232
  113.9 4.9 %collective-permute-start.22 = (f32[128,128]{1,0:T(8,128)S(1)}, f32[128,128]{1,0:T(8,128)S(1)}, u32[]{:S(2)}, u32[]{:S(2)}) collective-permute-start(f32[128,128]{1,0:T(8,128)S(1)} %embed_zl.1.refs_0_), channel_id=1, source_target_pairs={{0,1},{1,0},{2,3},{3,2},{4,5},{5,4},{6,7},{7,6},{8,9},{9,8},{10,11... | collective-permute-start | bytes 196616 | tf_op jit(solution)/shard_map/ppermute | solution.py:232
  (19 other events, 105.1 us)

commit v3 on v2

v3 whole, which is shorter than its diff:
```python
import jax
import jax.numpy as jnp
from jax import lax
from jax.experimental import pallas as pl
from jax.experimental.pallas import tpu as pltpu
from jax.sharding import PartitionSpec as P

SIDE = 4
CORES = 2
LANES = 128
ONES = 16
SCALE = 128.0
MIB = 2**20
F32 = jnp.float32
BF16 = jnp.bfloat16


def tile_lanes(column, width):
    return jnp.concatenate([column] * (width // LANES), axis=1)


def spread(row):
    return jnp.broadcast_to(row, (LANES, row.shape[1])).T


def four(refs):
    a, b, c, d = refs
    return (a[...] + b[...]) + (c[...] + d[...])


def block_rows(block, inner, core):
    return pl.ds(pl.multiple_of((block * CORES + core) * inner, inner), inner)


def kern_block(za, zn, ct, norms):
    cross = jnp.dot(za[...], ct, preferred_element_type=F32)
    return 1.0 / (cross + norms + tile_lanes(zn[...], ct.shape[1]))


def kern_setup(part, za, zn):
    zn[...] = jnp.broadcast_to(jnp.sum(part * part, axis=1, keepdims=True) + 1.0, zn.shape)
    za[...] = (-2.0 * part).astype(BF16)


def lane_sums(total, kern):
    for g in range(kern.shape[1] // LANES):
        total = total + kern[:, g * LANES : (g + 1) * LANES]
    return total


def own_body(z_ref, c_ref, kern_ref, row_ref, ct_ref, norm_ref, za, zn, buf, points, sems):
    half, count = kern_ref.shape
    inner = buf.shape[1]
    core = lax.axis_index("core")
    fetch = pltpu.make_async_copy(z_ref, points, sems.at[0])
    fetch.start()
    copies = [
        pltpu.make_async_copy(c_ref.at[block_rows(b, inner, core), :], buf.at[b], sems.at[b + 1])
        for b in range(count // inner)
    ]
    for copy in copies:
        copy.start()
    fetch.wait()
    kern_setup(points[...].astype(F32), za, zn)
    for copy in copies:
        copy.wait()
    total = jnp.zeros((half, LANES), F32)
    for b in range(count // inner):
        at = slice(b * inner, (b + 1) * inner)
        ct = buf[b].astype(F32).T
        norms = jnp.sum(ct * ct, axis=0, keepdims=True)
        ct = ct.astype(BF16)
        ct_ref[:, at] = ct
        norm_ref[:, at] = norms
        kern = kern_block(za, zn, ct, norms)
        kern_ref[:, at] = kern
        total = lane_sums(total, kern)
    row_ref[...] = jnp.sum(total.T, axis=0, keepdims=True)


def other_body(zo_ref, ct_ref, norm_ref, row_ref, kern_ref, rows_ref, za, zn):
    half, count = kern_ref.shape
    step = 256
    rows_ref[:1] = row_ref[...]
    kern_setup(zo_ref[...], za, zn)
    total = jnp.zeros((half, LANES), F32)
    for b in range(count // step):
        at = slice(b * step, (b + 1) * step)
        kern = kern_block(za, zn, ct_ref[:, at], norm_ref[:, at])
        kern_ref[:, at] = kern
        total = lane_sums(total, kern)
    rows_ref[1:] = jnp.sum(total.T, axis=0, keepdims=True)


def swap_add_body(mine, theirs, out):
    for n in range(out.shape[0]):
        out[n, :1] = mine[:1] + theirs[1:]
        out[n, 1:] = mine[1:] + theirs[:1]


def summed(ref):
    total = ref[0]
    for n in range(1, ref.shape[0]):
        total = total + ref[n]
    return total


def add_body(*refs):
    refs[-1][...] = four(refs[:-1]) if len(refs) == 5 else refs[0][...] + refs[1][...]


def freq_body(own_ref, other_ref, rows_ref, f_ref, rinv_ref):
    half, count = own_ref.shape
    rinv = 1.0 / summed(rows_ref)
    rinv_ref[...] = rinv
    parts = ((own_ref, spread(rinv[:1])), (other_ref, spread(rinv[1:])))
    for g in range(count // LANES):
        at = slice(g * LANES, (g + 1) * LANES)
        total = jnp.zeros((8, LANES), F32)
        for kern_ref, scale in parts:
            for i in range(0, half, 128):
                value = kern_ref[i : i + 128, at] * scale[i : i + 128]
                total = total + jnp.sum(value.reshape(16, 8, LANES), axis=0)
        f_ref[:, at] = jnp.sum(total, axis=0, keepdims=True)


def target_body(own_ref, other_ref, f0, f1, f2, f3, prior_ref, t_ref, finv_ref, acc):
    half, count = own_ref.shape
    inner = count // (SIDE * SIDE)
    core = lax.axis_index("core")
    prior = [prior_ref[:, block_rows(b, inner, core)] for b in range(count // inner)]
    finv_ref[...] = 1.0 / (four((f0, f1, f2, f3)) + jnp.concatenate(prior, axis=1))
    step = 64
    for row, kern_ref in ((0, own_ref), (1, other_ref)):
        for i in range(0, half, step):
            total = jnp.zeros((step, LANES), F32)
            for g in range(count // LANES):
                at = slice(g * LANES, (g + 1) * LANES)
                kern = kern_ref[i : i + step, at]
                total = total + kern * kern * finv_ref[:, at]
            acc[i : i + step] = total
        t_ref[row : row + 1] = jnp.sum(acc[...].T, axis=0, keepdims=True)


def weights(kern, finv, tinv, rinv):
    weight = kern * kern * (kern * finv * tinv - rinv)
    high = weight.astype(BF16)
    return high, (weight - high.astype(F32)).astype(BF16)


def grad_setup(tinv, rinv_ref, points, zt, ts, rs):
    for p in range(CORES):
        ts[p] = spread(tinv[p : p + 1])
        rs[p] = spread(rinv_ref[p : p + 1])
        zt[p, :LANES] = (-SCALE * points[p].T).astype(BF16)
        zt[p, LANES:] = jnp.full((ONES, points[p].shape[0]), SCALE, BF16)


def grad_piece(s, kerns, finv_ref, c_ref, zt, ts, rs, acc, piece):
    inner = piece.shape[1] // SIDE
    core, x = lax.axis_index("core"), lax.axis_index("x")
    for h in range(SIDE):
        block = (x ^ s) * SIDE + h
        at = pl.ds(pl.multiple_of(block * inner, inner), inner)
        c = c_ref[block_rows(block, inner, core), :]
        wide = jnp.concatenate([c, jnp.ones((inner, LANES), BF16)], axis=1)
        sums = jnp.zeros((LANES + ONES, inner), F32)
        for p in range(CORES):
            high, low = weights(
                kerns[p][:, at], finv_ref[:, at], tile_lanes(ts[p], inner), tile_lanes(rs[p], inner)
            )
            sums += jnp.dot(zt[p], high, preferred_element_type=F32)
            sums += jnp.dot(zt[p], low, preferred_element_type=F32)
            acc[p] += jnp.dot(high, wide, preferred_element_type=F32) + jnp.dot(
                low, wide, preferred_element_type=F32
            )
        piece[:, h * inner : (h + 1) * inner] = (
            sums[:LANES] + sums[LANES : LANES + 1] * c.astype(F32).T
        )


def far_body(own_ref, other_ref, rinv_ref, finv_ref, rows_ref, z_ref, zo_ref, c_ref, *outs):
    pieces, (tinv_ref, acc, zt, ts, rs) = outs[:3], outs[3:]
    points = (z_ref[...].astype(F32), zo_ref[...])
    tinv = 1.0 / summed(rows_ref)
    tinv_ref[...] = tinv
    grad_setup(tinv, rinv_ref, points, zt, ts, rs)
    acc[...] = jnp.zeros_like(acc)
    for s, piece in zip((1, 3, 2), pieces):
        grad_piece(s, (own_ref, other_ref), finv_ref, c_ref, zt, ts, rs, acc, piece)


def near_body(own_ref, other_ref, rinv_ref, finv_ref, tinv_ref, acc_ref, z_ref, zo_ref, c_ref, *outs):
    piece, own, other, zt, ts, rs, acc = outs
    points = (z_ref[...].astype(F32), zo_ref[...])
    grad_setup(tinv_ref[...], rinv_ref, points, zt, ts, rs)
    acc[...] = acc_ref[...]
    grad_piece(0, (own_ref, other_ref), finv_ref, c_ref, zt, ts, rs, acc, piece)
    for p, out in enumerate((own, other)):
        sums = acc[p]
        out[...] = SCALE * (sums[:, LANES:] * points[p] - sums[:, :LANES])


def split_body(near, far0, far1, far2, _, *outs):
    h = lax.axis_index("h")
    inner = outs[0].shape[1]
    for t in range(SIDE):
        at = pl.ds(pl.multiple_of((h ^ t) * inner, inner), inner)
        outs[t][...] = four([r.at[:, at] for r in (near, far0, far1, far2)])


def final_body(*refs):
    refs[SIDE][...] = four(refs[:SIDE]).T


VMEM = pl.BlockSpec(memory_space=pltpu.VMEM)
HBM = pl.BlockSpec(memory_space=pltpu.HBM)


def call(body, outs, *args, scratch=(), limit=2, name=None, flops=0, specs=None):
    shapes = tuple(o if hasattr(o, "dtype") else jax.ShapeDtypeStruct(o, F32) for o in outs)
    moved = sum(a.size * a.dtype.itemsize for a in args)
    out = pl.pallas_call(
        body,
        out_shape=shapes,
        in_specs=specs or [VMEM] * len(args),
        out_specs=tuple(VMEM for _ in outs),
        scratch_shapes=scratch,
        compiler_params=pltpu.CompilerParams(vmem_limit_bytes=limit * MIB),
        cost_estimate=pl.CostEstimate(flops=flops, bytes_accessed=moved, transcendentals=0),
        name=name,
    )(*args)
    return out if len(out) > 1 else out[0]


def swap(v, axis, s):
    return lax.ppermute(v, axis, [(i, i ^ s) for i in range(lax.axis_size(axis))])


def around(pieces, axis):
    return [pieces[0]] + [swap(pieces[s], axis, s) for s in (1, 3, 2)]


def body(embeddings, centres, prior_freq):
    half, width = embeddings.shape
    count = centres.shape[0] // CORES
    inner = count // (SIDE * SIDE)
    prior = prior_freq.reshape(1, centres.shape[0])
    rows = (CORES, half)

    def over_ctr(v):
        parts = lax.axis_size("zl") * lax.axis_size("y")
        v = call(swap_add_body, [(parts, *rows)], v, swap(v, "core", 1), name="sum_core")
        return lax.all_to_all(v, ("zl", "y"), 0, 0)

    z_other = swap(embeddings.astype(F32), "core", 1)
    kern_scratch = [pltpu.VMEM((half, width), BF16), pltpu.VMEM((half, LANES), F32)]
    kern_own, row, ct, norms = call(
        own_body,
        [(half, count), (1, half), jax.ShapeDtypeStruct((width, count), BF16), (1, count)],
        embeddings,
        centres,
        scratch=kern_scratch
        + [
            pltpu.VMEM((SIDE * SIDE, inner, width), BF16),
            pltpu.VMEM((half, width), BF16),
            pltpu.SemaphoreType.DMA((SIDE * SIDE + 1,)),
        ],
        limit=16,
        specs=[HBM, HBM],
        name="kern_own",
    )
    kern_other, row = call(
        other_body,
        [(half, count), rows],
        z_other,
        ct,
        norms,
        row,
        scratch=kern_scratch,
        limit=16,
        name="kern_other",
    )
    freq, rinv = call(
        freq_body,
        [(1, count), rows],
        kern_own,
        kern_other,
        over_ctr(row),
        limit=20,
        name="freq",
    )
    freq = call(add_body, [freq.shape], *around([freq] * SIDE, "x"), name="sum_x")
    target, finv = call(
        target_body,
        [rows, (1, count)],
        kern_own,
        kern_other,
        *around([freq] * SIDE, "h"),
        prior,
        scratch=[pltpu.VMEM((half, LANES), F32)],
        limit=20,
        name="target",
    )
    setup = [
        pltpu.VMEM((CORES, width + ONES, half), BF16),
        pltpu.VMEM((CORES, half, LANES), F32),
        pltpu.VMEM((CORES, half, LANES), F32),
    ]
    sums = (CORES, half, 2 * LANES)
    piece = (width, SIDE * inner)
    *far, tinv, acc = call(
        far_body,
        [piece] * 3 + [rows, sums],
        kern_own,
        kern_other,
        rinv,
        finv,
        over_ctr(target),
        embeddings,
        z_other,
        centres,
        scratch=setup,
        limit=24,
        name="grad_far",
    )
    far = [swap(v, "x", s) for v, s in zip(far, (1, 3, 2))]
    near, mine, other = call(
        near_body,
        [piece, (half, width), (half, width)],
        kern_own,
        kern_other,
        rinv,
        finv,
        tinv,
        acc,
        embeddings,
        z_other,
        centres,
        scratch=setup + [pltpu.VMEM(sums, F32)],
        limit=24,
        name="grad_near",
    )
    embed = call(add_body, [mine.shape], mine, swap(other, "core", 1), name="embed_core")
    embed = call(add_body, [mine.shape], embed, swap(embed, "zl", 1), name="embed_zl")
    by_h = call(
        split_body,
        [(width, inner)] * SIDE,
        near,
        *far,
        embed,
        specs=[VMEM] * SIDE + [pl.BlockSpec(memory_space=pl.ANY)],
        name="split",
    )
    embed = call(add_body, [mine.shape], embed, swap(embed, "y", 1), name="embed_y")
    embed = call(add_body, [mine.shape], embed, swap(embed, "y", 3), name="embed")
    grad = call(final_body, [(inner, width)], *around(by_h, "h"), name="final")
    return embed, grad.reshape(1, inner, width)


def solution(mesh):
    names = ("x", "h", "core", "zl", "y")
    grid = jax.sharding.Mesh(mesh.devices.reshape(SIDE, SIDE, CORES, CORES, SIDE), names)
    pts, ctr = names[:3], names[3:]
    in_specs = (P(pts, None), P(ctr, None), P(ctr))
    out_specs = (P(pts, None), P(ctr, pts, None))
    return jax.shard_map(body, mesh=grid, in_specs=in_specs, out_specs=out_specs, check_vma=False)
```

time: 120 us -> 112 us (0.933)
  starting transfers between devices: 59.4 us -> 27.3 us
  blocking collectives: 0 us -> 19.2 us
  waiting for transfers between devices: 36.7 us -> 41.8 us
  Pallas kernels: 17.6 us -> 19.4 us
  local copies, waits for them, and re-layouts: 4.09 us -> 2.5 us
    ppermute x37 -> x19, starting transfers between devices: 59.4 us -> 27.3 us  [swap(): lax.ppermute(v, axis, [(i, i ^ s) for i in range(lax.axis_size(axis))])]
    all_to_all x0 -> x2, blocking collectives: none -> 19.2 us  [over_ctr(): return lax.all_to_all(v, ('zl', 'y'), 0, 0)]
    ppermute x37 -> x19, waiting for transfers between devices: 36.7 us -> 41.8 us  [swap(): lax.ppermute(v, axis, [(i, i ^ s) for i in range(lax.axis_size(axis))])]
    pallas_call x17 -> x15, Pallas kernels: 17.6 us -> 19.4 us  [call(): pl.pallas_call(body, out_shape=shapes, in_specs=specs or [VMEM] * len(arg...]
    unnamed x12 -> x10, local copies, waits for them, and re-layouts: 4.09 us -> 2.5 us
  transfers between devices with their start and end apart: 37 -> 19, of which waited for: 19 -> 14; matrix products, arithmetic and copies ran while one was open for 0% -> 0% of each run, Pallas kernels for 3% -> 5%
where the time goes in v3:
time: 112 us
  waiting for transfers between devices  41.8 us (37%)
  starting transfers between devices  27.3 us (24%)
  Pallas kernels  19.4 us (17%)
  blocking collectives  19.2 us (17%)
  local copies, waits for them, and re-layouts  2.5 us (2%)
    ppermute x19, waiting for transfers between devices, swap(): lax.ppermute(v, axis, [(i, i ^ s) for i in range(lax.axis_size(axis))])  41.8 us
    ppermute x19, starting transfers between devices, swap(): lax.ppermute(v, axis, [(i, i ^ s) for i in range(lax.axis_size(axis))])  27.3 us
    pallas_call x15, Pallas kernels, call(): pl.pallas_call(body, out_shape=shapes, in_specs=specs or [VMEM] * len(arg...  19.4 us
    all_to_all x2, blocking collectives, over_ctr(): return lax.all_to_all(v, ('zl', 'y'), 0, 0)  19.2 us
    unnamed x10, local copies, waits for them, and re-layouts  2.5 us
  transfers between devices with their start and end apart: 19, of which 14 were waited for; matrix products, arithmetic and copies ran while one was open for 0% of the time, Pallas kernels for 5%

profile of v3, /device:TPU:32, one launch (start us, length us, event | category | flops | bytes accessed | tf_op | source)
XLA Modules:
  0.0 111.8 jit_solution(6849777621438475915)
XLA Ops:
  1.7 1.6 %copy-done = bf16[8192,128]{1,0:T(8,128)(2,1)S(1)} copy-done((bf16[8192,128]{1,0:T(8,128)(2,1)S(1)}, bf16[8192,128]{1,0:T(8,128)(2,1)}, u32[]{:S(2)}) %copy-start) | copy-done | bytes 2097176
  4.2 4.1 %kern_own.1 = (f32[512,4096]{1,0:T(8,128)S(1)}, f32[1,512]{1,0:T(1,128)S(1)}, bf16[128,4096]{1,0:T(8,128)(2,1)S(1)}, f32[1,4096]{1,0:T(1,128)S(1)}) custom-call(bf16[512,128]{1,0:T(8,128)(2,1)S(1)} %copy-done.2, bf16[8192,128]{1,0:T(8,128)(2,1)S(1)} %copy-done), custom_call_target="tpu_custom_call" | custom-call | bytes 2228224 | tf_op jit(solution)/shard_map/kern_own/pallas_call | solution.py:223
  8.3 1.7 %kern_other.1 = (f32[512,4096]{1,0:T(8,128)S(1)}, f32[2,512]{1,0:T(2,128)S(1)}) custom-call(f32[512,128]{1,0:T(8,128)S(1)} %collective-permute-done.zo_ref, bf16[128,4096]{1,0:T(8,128)(2,1)S(1)} %get-tuple-element.25.ct_ref, f32[1,4096]{1,0:T(1,128)S(1)} %get-tuple-element.26.norm_ref, f32[1,512]{1,0:T(1,128)S(1)} %get-tuple-element.27.row_ref), custom_call_target="tpu_custom_call" | custom-call | bytes 1329152 | tf_op jit(solution)/shard_map/kern_other/pallas_call | solution.py:223
  11.4 10.6 %all_to_all.10.rows_ref = f32[8,2,512]{2,1,0:T(2,128)S(1)} all-to-all(f32[8,2,512]{2,1,0:T(2,128)S(1)} %sum_core.2), channel_id=1, replica_groups=mesh['x'=4,'h'=4,'core'=2,'zl'=2,'y'=4] {'zl','y'}, dimensions={0} | all-to-all | bytes 65536 | tf_op jit(solution)/shard_map/all_to_all | solution.py:254
  21.9 1.7 %freq.1 = (f32[1,4096]{1,0:T(1,128)S(1)}, f32[2,512]{1,0:T(2,128)S(1)}) custom-call(f32[512,4096]{1,0:T(8,128)S(1)} %get-tuple-element.24.own_ref, f32[512,4096]{1,0:T(8,128)S(1)} %get-tuple-element.28.other_ref, f32[8,2,512]{2,1,0:T(2,128)S(1)} %all_to_all.10.rows_ref), custom_call_target="tpu_custom_call" | custom-call | bytes 16809984 | tf_op jit(solution)/shard_map/freq/pallas_call | solution.py:223
  23.6 3.1 %collective-permute-start.4 = (f32[1,4096]{1,0:T(1,128)S(1)}, f32[1,4096]{1,0:T(1,128)S(1)}, u32[]{:S(2)}, u32[]{:S(2)}) collective-permute-start(f32[1,4096]{1,0:T(1,128)S(1)} %get-tuple-element.31.refs_0_), channel_id=1, source_target_pairs={{0,128},{64,192},{128,0},{192,64},{1,129},{65,193},{129,1},{193,65... | collective-permute-start | bytes 49160 | tf_op jit(solution)/shard_map/ppermute | solution.py:237
  28.9 2.7 %collective-permute-done.3.refs_2_ = f32[1,4096]{1,0:T(1,128)S(1)} collective-permute-done((f32[1,4096]{1,0:T(1,128)S(1)}, f32[1,4096]{1,0:T(1,128)S(1)}, u32[]{:S(2)}, u32[]{:S(2)}) %collective-permute-start.3) | collective-permute-done | bytes 16416 | tf_op jit(solution)/shard_map/ppermute | solution.py:237
  31.7 6.4 %collective-permute-start.7 = (f32[1,4096]{1,0:T(1,128)S(1)}, f32[1,4096]{1,0:T(1,128)S(1)}, u32[]{:S(2)}, u32[]{:S(2)}) collective-permute-start(f32[1,4096]{1,0:T(1,128)S(1)} %sum_x.1.f0), channel_id=1, source_target_pairs={{0,32},{16,48},{32,0},{48,16},{1,33},{17,49},{33,1},{49,17},{2,34}... | collective-permute-start | bytes 49160 | tf_op jit(solution)/shard_map/ppermute | solution.py:237
  39.8 4.1 %collective-permute-done.6.f2 = f32[1,4096]{1,0:T(1,128)S(1)} collective-permute-done((f32[1,4096]{1,0:T(1,128)S(1)}, f32[1,4096]{1,0:T(1,128)S(1)}, u32[]{:S(2)}, u32[]{:S(2)}) %collective-permute-start.6) | collective-permute-done | bytes 16416 | tf_op jit(solution)/shard_map/ppermute | solution.py:237
  43.9 1.9 %target.1 = (f32[2,512]{1,0:T(2,128)S(1)}, f32[1,4096]{1,0:T(1,128)S(1)}) custom-call(f32[512,4096]{1,0:T(8,128)S(1)} %get-tuple-element.24.own_ref, f32[512,4096]{1,0:T(8,128)S(1)} %get-tuple-element.28.other_ref, f32[1,4096]{1,0:T(1,128)S(1)} %sum_x.1.f0, f32[1,4096]{1,0:T(1,128)S(1)} %collective-permute-done.5.f1, ...), custom_call_target="tpu_custom_call" | custom-call | bytes 16875520 | tf_op jit(solution)/shard_map/target/pallas_call | solution.py:223
  47.3 8.6 %all_to_all.11.rows_ref = f32[8,2,512]{2,1,0:T(2,128)S(1)} all-to-all(f32[8,2,512]{2,1,0:T(2,128)S(1)} %sum_core.3), channel_id=1, replica_groups=mesh['x'=4,'h'=4,'core'=2,'zl'=2,'y'=4] {'zl','y'}, dimensions={0} | all-to-all | bytes 65536 | tf_op jit(solution)/shard_map/all_to_all | solution.py:254
  55.9 5.9 %grad_far.1 = (f32[128,1024]{1,0:T(8,128)S(1)}, f32[128,1024]{1,0:T(8,128)S(1)}, f32[128,1024]{1,0:T(8,128)S(1)}, f32[2,512]{1,0:T(2,128)S(1)}, f32[2,512,256]{2,1,0:T(8,128)S(1)}) custom-call(f32[512,4096]{1,0:T(8,128)S(1)} %get-tuple-element.24.own_ref, f32[512,4096]{1,0:T(8,128)S(1)} %get-tuple-element.28.other_ref, ...), custom_call_target="tpu_custom_call" | custom-call | bytes 19320832 | tf_op jit(solution)/shard_map/grad_far/pallas_call | solution.py:223
  61.9 2.3 %grad_near.1 = (f32[128,1024]{1,0:T(8,128)S(1)}, f32[512,128]{1,0:T(8,128)S(1)}, f32[512,128]{1,0:T(8,128)S(1)}) custom-call(f32[512,4096]{1,0:T(8,128)S(1)} %get-tuple-element.24.own_ref, f32[512,4096]{1,0:T(8,128)S(1)} %get-tuple-element.28.other_ref, f32[2,512]{1,0:T(2,128)S(1)} %get-tuple-element.30.rinv_ref, f32[1,4096]{1,0:T(1,128)S(1)} %get-tuple-element.32.finv_ref, ...), custom_call_target="tpu_custom_call" | custom-call | bytes 20340736 | tf_op jit(solution)/shard_map/grad_near/pallas_call | solution.py:223
  67.3 2.0 %collective-permute-start.14 = (f32[128,1024]{1,0:T(8,128)S(1)}, f32[128,1024]{1,0:T(8,128)S(1)}, u32[]{:S(2)}, u32[]{:S(2)}) collective-permute-start(f32[128,1024]{1,0:T(8,128)S(1)} %get-tuple-element.40), channel_id=1, source_target_pairs={{0,192},{64,128},{128,64},{192,0},{1,193},{65,129},{129,65},{193,1... | collective-permute-start | bytes 1572872 | tf_op jit(solution)/shard_map/ppermute | solution.py:237
  69.4 2.1 %collective-permute-start.15 = (f32[128,1024]{1,0:T(8,128)S(1)}, f32[128,1024]{1,0:T(8,128)S(1)}, u32[]{:S(2)}, u32[]{:S(2)}) collective-permute-start(f32[128,1024]{1,0:T(8,128)S(1)} %get-tuple-element.41), channel_id=1, source_target_pairs={{0,128},{64,192},{128,0},{192,64},{1,129},{65,193},{129,1},{193,65... | collective-permute-start | bytes 1572872 | tf_op jit(solution)/shard_map/ppermute | solution.py:237
  71.4 2.8 %collective-permute-done.10.refs_1_ = f32[512,128]{1,0:T(8,128)S(1)} collective-permute-done((f32[512,128]{1,0:T(8,128)S(1)}, f32[512,128]{1,0:T(8,128)S(1)}, u32[]{:S(2)}, u32[]{:S(2)}) %collective-permute-start.10) | collective-permute-done | bytes 262176 | tf_op jit(solution)/shard_map/ppermute | solution.py:237
  75.0 6.9 %collective-permute-done.11.refs_1_ = f32[512,128]{1,0:T(8,128)S(1)} collective-permute-done((f32[512,128]{1,0:T(8,128)S(1)}, f32[512,128]{1,0:T(8,128)S(1)}, u32[]{:S(2)}, u32[]{:S(2)}) %collective-permute-start.11) | collective-permute-done | bytes 262176 | tf_op jit(solution)/shard_map/ppermute | solution.py:237
  83.2 8.6 %collective-permute-done.14.far1 = f32[128,1024]{1,0:T(8,128)S(1)} collective-permute-done((f32[128,1024]{1,0:T(8,128)S(1)}, f32[128,1024]{1,0:T(8,128)S(1)}, u32[]{:S(2)}, u32[]{:S(2)}) %collective-permute-start.14) | collective-permute-done | bytes 524320 | tf_op jit(solution)/shard_map/ppermute | solution.py:237
  91.8 1.9 %collective-permute-done.15.far2 = f32[128,1024]{1,0:T(8,128)S(1)} collective-permute-done((f32[128,1024]{1,0:T(8,128)S(1)}, f32[128,1024]{1,0:T(8,128)S(1)}, u32[]{:S(2)}, u32[]{:S(2)}) %collective-permute-start.15) | collective-permute-done | bytes 524320 | tf_op jit(solution)/shard_map/ppermute | solution.py:237
  93.8 1.7 %collective-permute-start.16 = (f32[128,256]{1,0:T(8,128)S(1)}, f32[128,256]{1,0:T(8,128)S(1)}, u32[]{:S(2)}, u32[]{:S(2)}) collective-permute-start(f32[128,256]{1,0:T(8,128)S(1)} %get-tuple-element.43), channel_id=1, source_target_pairs={{0,16},{16,0},{32,48},{48,32},{1,17},{17,1},{33,49},{49,33},{2,18}... | collective-permute-start | bytes 393224 | tf_op jit(solution)/shard_map/ppermute | solution.py:237
  95.6 2.9 %collective-permute-start.17 = (f32[128,256]{1,0:T(8,128)S(1)}, f32[128,256]{1,0:T(8,128)S(1)}, u32[]{:S(2)}, u32[]{:S(2)}) collective-permute-start(f32[128,256]{1,0:T(8,128)S(1)} %get-tuple-element.44), channel_id=1, source_target_pairs={{0,48},{16,32},{32,16},{48,0},{1,49},{17,33},{33,17},{49,1},{2,50}... | collective-permute-start | bytes 393224 | tf_op jit(solution)/shard_map/ppermute | solution.py:237
  98.5 1.9 %collective-permute-start.18 = (f32[128,256]{1,0:T(8,128)S(1)}, f32[128,256]{1,0:T(8,128)S(1)}, u32[]{:S(2)}, u32[]{:S(2)}) collective-permute-start(f32[128,256]{1,0:T(8,128)S(1)} %get-tuple-element.45), channel_id=1, source_target_pairs={{0,32},{16,48},{32,0},{48,16},{1,33},{17,49},{33,1},{49,17},{2,34}... | collective-permute-start | bytes 393224 | tf_op jit(solution)/shard_map/ppermute | solution.py:237
  101.7 3.3 %collective-permute-done.17.refs_2_ = f32[128,256]{1,0:T(8,128)S(1)} collective-permute-done((f32[128,256]{1,0:T(8,128)S(1)}, f32[128,256]{1,0:T(8,128)S(1)}, u32[]{:S(2)}, u32[]{:S(2)}) %collective-permute-start.17) | collective-permute-done | bytes 131104 | tf_op jit(solution)/shard_map/ppermute | solution.py:237
  105.1 5.2 %collective-permute-done.18.refs_3_ = f32[128,256]{1,0:T(8,128)S(1)} collective-permute-done((f32[128,256]{1,0:T(8,128)S(1)}, f32[128,256]{1,0:T(8,128)S(1)}, u32[]{:S(2)}, u32[]{:S(2)}) %collective-permute-start.18) | collective-permute-done | bytes 131104 | tf_op jit(solution)/shard_map/ppermute | solution.py:237
  (42 shorter events, 16.8 us)
Async XLA Ops:
  1.6 6.7 %collective-permute-start = (f32[512,128]{1,0:T(8,128)S(1)}, f32[512,128]{1,0:T(8,128)S(1)}, u32[]{:S(2)}, u32[]{:S(2)}) collective-permute-start(f32[512,128]{1,0:T(8,128)S(1)} %convert_element_type.3), channel_id=1, source_target_pairs={{0,8},{8,0},{1,9},{9,1},{2,10},{10,2},{3,11},{11,3},{4,12},{12,4},... | collective-permute-start | bytes 786440 | tf_op jit(solution)/shard_map/ppermute | solution.py:237
  1.7 1.6 %copy-start = (bf16[8192,128]{1,0:T(8,128)(2,1)S(1)}, bf16[8192,128]{1,0:T(8,128)(2,1)}, u32[]{:S(2)}) copy-start(bf16[8192,128]{1,0:T(8,128)(2,1)} %c_ref.5) | copy-start | bytes 6291460
  3.3 0.9 copy-start.2
  10.0 1.4 %collective-permute-start.1 = (f32[2,512]{1,0:T(2,128)S(1)}, f32[2,512]{1,0:T(2,128)S(1)}, u32[]{:S(2)}, u32[]{:S(2)}) collective-permute-start(f32[2,512]{1,0:T(2,128)S(1)} %get-tuple-element.29.mine), channel_id=1, source_target_pairs={{0,8},{8,0},{1,9},{9,1},{2,10},{10,2},{3,11},{11,3},{4,12},{12,4},... | collective-permute-start | bytes 12296 | tf_op jit(solution)/shard_map/ppermute | solution.py:237
  21.9 22.0 %copy-start.4 = (f32[8192]{0:T(1024)S(1)}, f32[8192]{0:T(1024)}, u32[]{:S(2)}) copy-start(f32[8192]{0:T(1024)} %param.5) | copy-start | bytes 98308
  23.6 5.3 %collective-permute-start.4 = (f32[1,4096]{1,0:T(1,128)S(1)}, f32[1,4096]{1,0:T(1,128)S(1)}, u32[]{:S(2)}, u32[]{:S(2)}) collective-permute-start(f32[1,4096]{1,0:T(1,128)S(1)} %get-tuple-element.31.refs_0_), channel_id=1, source_target_pairs={{0,128},{64,192},{128,0},{192,64},{1,129},{65,193},{129,1},{193,65... | collective-permute-start | bytes 49160 | tf_op jit(solution)/shard_map/ppermute | solution.py:237
  26.7 4.9 %collective-permute-start.3 = (f32[1,4096]{1,0:T(1,128)S(1)}, f32[1,4096]{1,0:T(1,128)S(1)}, u32[]{:S(2)}, u32[]{:S(2)}) collective-permute-start(f32[1,4096]{1,0:T(1,128)S(1)} %get-tuple-element.31.refs_0_), channel_id=1, source_target_pairs={{0,192},{64,128},{128,64},{192,0},{1,193},{65,129},{129,65},{193,1... | collective-permute-start | bytes 49160 | tf_op jit(solution)/shard_map/ppermute | solution.py:237
  27.9 3.8 %collective-permute-start.2 = (f32[1,4096]{1,0:T(1,128)S(1)}, f32[1,4096]{1,0:T(1,128)S(1)}, u32[]{:S(2)}, u32[]{:S(2)}) collective-permute-start(f32[1,4096]{1,0:T(1,128)S(1)} %get-tuple-element.31.refs_0_), channel_id=1, source_target_pairs={{0,64},{64,0},{128,192},{192,128},{1,65},{65,1},{129,193},{193,129... | collective-permute-start | bytes 49160 | tf_op jit(solution)/shard_map/ppermute | solution.py:237
  31.7 8.1 %collective-permute-start.7 = (f32[1,4096]{1,0:T(1,128)S(1)}, f32[1,4096]{1,0:T(1,128)S(1)}, u32[]{:S(2)}, u32[]{:S(2)}) collective-permute-start(f32[1,4096]{1,0:T(1,128)S(1)} %sum_x.1.f0), channel_id=1, source_target_pairs={{0,32},{16,48},{32,0},{48,16},{1,33},{17,49},{33,1},{49,17},{2,34}... | collective-permute-start | bytes 49160 | tf_op jit(solution)/shard_map/ppermute | solution.py:237
  38.1 5.8 %collective-permute-start.6 = (f32[1,4096]{1,0:T(1,128)S(1)}, f32[1,4096]{1,0:T(1,128)S(1)}, u32[]{:S(2)}, u32[]{:S(2)}) collective-permute-start(f32[1,4096]{1,0:T(1,128)S(1)} %sum_x.1.f0), channel_id=1, source_target_pairs={{0,48},{16,32},{32,16},{48,0},{1,49},{17,33},{33,17},{49,1},{2,50}... | collective-permute-start | bytes 49160 | tf_op jit(solution)/shard_map/ppermute | solution.py:237
  38.6 5.3 %collective-permute-start.5 = (f32[1,4096]{1,0:T(1,128)S(1)}, f32[1,4096]{1,0:T(1,128)S(1)}, u32[]{:S(2)}, u32[]{:S(2)}) collective-permute-start(f32[1,4096]{1,0:T(1,128)S(1)} %sum_x.1.f0), channel_id=1, source_target_pairs={{0,16},{16,0},{32,48},{48,32},{1,17},{17,1},{33,49},{49,33},{2,18}... | collective-permute-start | bytes 49160 | tf_op jit(solution)/shard_map/ppermute | solution.py:237
  43.9 12.0 %copy-start.1 = (bf16[8192,128]{1,0:T(8,128)(2,1)S(1)}, bf16[8192,128]{1,0:T(8,128)(2,1)}, u32[]{:S(2)}) copy-start(bf16[8192,128]{1,0:T(8,128)(2,1)} %c_ref.5) | copy-start | bytes 6291460
  43.9 12.0 %copy-start.3 = (bf16[512,128]{1,0:T(8,128)(2,1)S(1)}, bf16[512,128]{1,0:T(8,128)(2,1)}, u32[]{:S(2)}) copy-start(bf16[512,128]{1,0:T(8,128)(2,1)} %z_ref.5) | copy-start | bytes 393220
  45.8 1.4 %collective-permute-start.8 = (f32[2,512]{1,0:T(2,128)S(1)}, f32[2,512]{1,0:T(2,128)S(1)}, u32[]{:S(2)}, u32[]{:S(2)}) collective-permute-start(f32[2,512]{1,0:T(2,128)S(1)} %get-tuple-element.33.mine), channel_id=1, source_target_pairs={{0,8},{8,0},{1,9},{9,1},{2,10},{10,2},{3,11},{11,3},{4,12},{12,4},... | collective-permute-start | bytes 12296 | tf_op jit(solution)/shard_map/ppermute | solution.py:237
  64.2 1.6 %collective-permute-start.9 = (f32[512,128]{1,0:T(8,128)S(1)}, f32[512,128]{1,0:T(8,128)S(1)}, u32[]{:S(2)}, u32[]{:S(2)}) collective-permute-start(f32[512,128]{1,0:T(8,128)S(1)} %get-tuple-element.37), channel_id=1, source_target_pairs={{0,8},{8,0},{1,9},{9,1},{2,10},{10,2},{3,11},{11,3},{4,12},{12,4},... | collective-permute-start | bytes 786440 | tf_op jit(solution)/shard_map/ppermute | solution.py:237
  65.8 8.4 %collective-permute-start.10 = (f32[512,128]{1,0:T(8,128)S(1)}, f32[512,128]{1,0:T(8,128)S(1)}, u32[]{:S(2)}, u32[]{:S(2)}) collective-permute-start(f32[512,128]{1,0:T(8,128)S(1)} %embed_core.1.refs_0_), channel_id=1, source_target_pairs={{0,4},{4,0},{1,5},{5,1},{2,6},{6,2},{3,7},{7,3},{8,12},{12,8},{9,1... | collective-permute-start | bytes 786440 | tf_op jit(solution)/shard_map/ppermute | solution.py:237
  67.3 15.9 %collective-permute-start.13 = (f32[128,1024]{1,0:T(8,128)S(1)}, f32[128,1024]{1,0:T(8,128)S(1)}, u32[]{:S(2)}, u32[]{:S(2)}) collective-permute-start(f32[128,1024]{1,0:T(8,128)S(1)} %get-tuple-element.39), channel_id=1, source_target_pairs={{0,64},{64,0},{128,192},{192,128},{1,65},{65,1},{129,193},{193,129... | collective-permute-start | bytes 1572872 | tf_op jit(solution)/shard_map/ppermute | solution.py:237
  67.3 24.5 %collective-permute-start.14 = (f32[128,1024]{1,0:T(8,128)S(1)}, f32[128,1024]{1,0:T(8,128)S(1)}, u32[]{:S(2)}, u32[]{:S(2)}) collective-permute-start(f32[128,1024]{1,0:T(8,128)S(1)} %get-tuple-element.40), channel_id=1, source_target_pairs={{0,192},{64,128},{128,64},{192,0},{1,193},{65,129},{129,65},{193,1... | collective-permute-start | bytes 1572872 | tf_op jit(solution)/shard_map/ppermute | solution.py:237
  69.4 24.4 %collective-permute-start.15 = (f32[128,1024]{1,0:T(8,128)S(1)}, f32[128,1024]{1,0:T(8,128)S(1)}, u32[]{:S(2)}, u32[]{:S(2)}) collective-permute-start(f32[128,1024]{1,0:T(8,128)S(1)} %get-tuple-element.41), channel_id=1, source_target_pairs={{0,128},{64,192},{128,0},{192,64},{1,129},{65,193},{129,1},{193,65... | collective-permute-start | bytes 1572872 | tf_op jit(solution)/shard_map/ppermute | solution.py:237
  74.3 7.6 %collective-permute-start.11 = (f32[512,128]{1,0:T(8,128)S(1)}, f32[512,128]{1,0:T(8,128)S(1)}, u32[]{:S(2)}, u32[]{:S(2)}) collective-permute-start(f32[512,128]{1,0:T(8,128)S(1)} %embed_zl.1.refs_0_._), channel_id=1, source_target_pairs={{0,1},{1,0},{2,3},{3,2},{4,5},{5,4},{6,7},{7,6},{8,9},{9,8},{10,11... | collective-permute-start | bytes 786440 | tf_op jit(solution)/shard_map/ppermute | solution.py:237
  81.9 29.1 %collective-permute-start.12 = (f32[512,128]{1,0:T(8,128)S(1)}, f32[512,128]{1,0:T(8,128)S(1)}, u32[]{:S(2)}, u32[]{:S(2)}) collective-permute-start(f32[512,128]{1,0:T(8,128)S(1)} %embed_y.1.refs_0_), channel_id=1, source_target_pairs={{0,3},{1,2},{2,1},{3,0},{4,7},{5,6},{6,5},{7,4},{8,11},{9,10},{10,... | collective-permute-start | bytes 786440 | tf_op jit(solution)/shard_map/ppermute | solution.py:237
  93.8 7.9 %collective-permute-start.16 = (f32[128,256]{1,0:T(8,128)S(1)}, f32[128,256]{1,0:T(8,128)S(1)}, u32[]{:S(2)}, u32[]{:S(2)}) collective-permute-start(f32[128,256]{1,0:T(8,128)S(1)} %get-tuple-element.43), channel_id=1, source_target_pairs={{0,16},{16,0},{32,48},{48,32},{1,17},{17,1},{33,49},{49,33},{2,18}... | collective-permute-start | bytes 393224 | tf_op jit(solution)/shard_map/ppermute | solution.py:237
  95.6 9.5 %collective-permute-start.17 = (f32[128,256]{1,0:T(8,128)S(1)}, f32[128,256]{1,0:T(8,128)S(1)}, u32[]{:S(2)}, u32[]{:S(2)}) collective-permute-start(f32[128,256]{1,0:T(8,128)S(1)} %get-tuple-element.44), channel_id=1, source_target_pairs={{0,48},{16,32},{32,16},{48,0},{1,49},{17,33},{33,17},{49,1},{2,50}... | collective-permute-start | bytes 393224 | tf_op jit(solution)/shard_map/ppermute | solution.py:237
  98.5 11.8 %collective-permute-start.18 = (f32[128,256]{1,0:T(8,128)S(1)}, f32[128,256]{1,0:T(8,128)S(1)}, u32[]{:S(2)}, u32[]{:S(2)}) collective-permute-start(f32[128,256]{1,0:T(8,128)S(1)} %get-tuple-element.45), channel_id=1, source_target_pairs={{0,32},{16,48},{32,0},{48,16},{1,33},{17,49},{33,1},{49,17},{2,34}... | collective-permute-start | bytes 393224 | tf_op jit(solution)/shard_map/ppermute | solution.py:237

commit v4 on v3

--- a/solution.py
+++ b/solution.py
@@ -11,6 +11,7 @@
 ONES = 16
 SCALE = 128.0
 MIB = 2**20
+HINT = 10**10
 F32 = jnp.float32
 BF16 = jnp.bfloat16
 
@@ -48,26 +49,15 @@
     return total
 
 
-def own_body(z_ref, c_ref, kern_ref, row_ref, ct_ref, norm_ref, za, zn, buf, points, sems):
+def own_body(z_ref, c_ref, kern_ref, row_ref, ct_ref, norm_ref, za, zn):
     half, count = kern_ref.shape
-    inner = buf.shape[1]
+    inner = count // (SIDE * SIDE)
     core = lax.axis_index("core")
-    fetch = pltpu.make_async_copy(z_ref, points, sems.at[0])
-    fetch.start()
-    copies = [
-        pltpu.make_async_copy(c_ref.at[block_rows(b, inner, core), :], buf.at[b], sems.at[b + 1])
-        for b in range(count // inner)
-    ]
-    for copy in copies:
-        copy.start()
-    fetch.wait()
-    kern_setup(points[...].astype(F32), za, zn)
-    for copy in copies:
-        copy.wait()
+    kern_setup(z_ref[...], za, zn)
     total = jnp.zeros((half, LANES), F32)
     for b in range(count // inner):
         at = slice(b * inner, (b + 1) * inner)
-        ct = buf[b].astype(F32).T
+        ct = c_ref[block_rows(b, inner, core), :].astype(F32).T
         norms = jnp.sum(ct * ct, axis=0, keepdims=True)
         ct = ct.astype(BF16)
         ct_ref[:, at] = ct
@@ -156,57 +146,81 @@
         zt[p, LANES:] = jnp.full((ONES, points[p].shape[0]), SCALE, BF16)
 
 
-def grad_piece(s, kerns, finv_ref, c_ref, zt, ts, rs, acc, piece):
-    inner = piece.shape[1] // SIDE
-    core, x = lax.axis_index("core"), lax.axis_index("x")
-    for h in range(SIDE):
-        block = (x ^ s) * SIDE + h
-        at = pl.ds(pl.multiple_of(block * inner, inner), inner)
-        c = c_ref[block_rows(block, inner, core), :]
-        wide = jnp.concatenate([c, jnp.ones((inner, LANES), BF16)], axis=1)
-        sums = jnp.zeros((LANES + ONES, inner), F32)
-        for p in range(CORES):
-            high, low = weights(
-                kerns[p][:, at], finv_ref[:, at], tile_lanes(ts[p], inner), tile_lanes(rs[p], inner)
-            )
-            sums += jnp.dot(zt[p], high, preferred_element_type=F32)
-            sums += jnp.dot(zt[p], low, preferred_element_type=F32)
-            acc[p] += jnp.dot(high, wide, preferred_element_type=F32) + jnp.dot(
-                low, wide, preferred_element_type=F32
-            )
-        piece[:, h * inner : (h + 1) * inner] = (
-            sums[:LANES] + sums[LANES : LANES + 1] * c.astype(F32).T
-        )
+def grad_weights(block, kerns, finv_ref, ts, rs, p):
+    inner = kerns[p].shape[1] // (SIDE * SIDE)
+    at = pl.ds(pl.multiple_of(block * inner, inner), inner)
+    return weights(
+        kerns[p][:, at], finv_ref[:, at], tile_lanes(ts[p], inner), tile_lanes(rs[p], inner)
+    )
+
+
+def grad_block(parts, zt, c):
+    sums = jnp.zeros((LANES + ONES, c.shape[0]), F32)
+    for p, terms in enumerate(parts):
+        for term in terms:
+            sums += jnp.dot(zt[p], term, preferred_element_type=F32)
+    return sums[:LANES] + sums[LANES : LANES + 1] * c.astype(F32).T
 
 
 def far_body(own_ref, other_ref, rinv_ref, finv_ref, rows_ref, z_ref, zo_ref, c_ref, *outs):
-    pieces, (tinv_ref, acc, zt, ts, rs) = outs[:3], outs[3:]
+    first, third, keep1, keep3, tinv_ref, zt, ts, rs = outs
+    kerns = (own_ref, other_ref)
     points = (z_ref[...].astype(F32), zo_ref[...])
     tinv = 1.0 / summed(rows_ref)
     tinv_ref[...] = tinv
     grad_setup(tinv, rinv_ref, points, zt, ts, rs)
-    acc[...] = jnp.zeros_like(acc)
-    for s, piece in zip((1, 3, 2), pieces):
-        grad_piece(s, (own_ref, other_ref), finv_ref, c_ref, zt, ts, rs, acc, piece)
-
-
-def near_body(own_ref, other_ref, rinv_ref, finv_ref, tinv_ref, acc_ref, z_ref, zo_ref, c_ref, *outs):
+    core, x = lax.axis_index("core"), lax.axis_index("x")
+    cut, wide = keep1.shape
+    inner = wide // SIDE
+    targets = {1: (first, 0, keep1, 0), 3: (keep3, 0, third, 0), 2: (first, wide, third, wide)}
+    for s, (low, low_at, high, high_at) in targets.items():
+        for h in range(SIDE):
+            block = (x ^ s) * SIDE + h
+            parts = [grad_weights(block, kerns, finv_ref, ts, rs, p) for p in range(CORES)]
+            grad = grad_block(parts, zt, c_ref[block_rows(block, inner, core), :])
+            low[:, low_at + h * inner : low_at + (h + 1) * inner] = grad[:cut]
+            high[:, high_at + h * inner : high_at + (h + 1) * inner] = grad[cut:]
+
+
+def near_body(own_ref, other_ref, rinv_ref, finv_ref, tinv_ref, z_ref, zo_ref, c_ref, *outs):
     piece, own, other, zt, ts, rs, acc = outs
+    kerns = (own_ref, other_ref)
     points = (z_ref[...].astype(F32), zo_ref[...])
     grad_setup(tinv_ref[...], rinv_ref, points, zt, ts, rs)
-    acc[...] = acc_ref[...]
-    grad_piece(0, (own_ref, other_ref), finv_ref, c_ref, zt, ts, rs, acc, piece)
+    acc[...] = jnp.zeros_like(acc)
+    core, x = lax.axis_index("core"), lax.axis_index("x")
+    inner = piece.shape[1] // SIDE
+    for s in range(SIDE):
+        for h in range(SIDE):
+            block = (x ^ s) * SIDE + h
+            c = c_ref[block_rows(block, inner, core), :]
+            wide = jnp.concatenate([c, jnp.ones((inner, LANES), BF16)], axis=1)
+            parts = [grad_weights(block, kerns, finv_ref, ts, rs, p) for p in range(CORES)]
+            for p, (high, low) in enumerate(parts):
+                acc[p] += jnp.dot(high, wide, preferred_element_type=F32) + jnp.dot(
+                    low, wide, preferred_element_type=F32
+                )
+            if s == 0:
+                piece[:, h * inner : (h + 1) * inner] = grad_block(parts, zt, c)
     for p, out in enumerate((own, other)):
         sums = acc[p]
         out[...] = SCALE * (sums[:, LANES:] * points[p] - sums[:, :LANES])
 
 
-def split_body(near, far0, far1, far2, _, *outs):
+def second_body(keep1, keep3, first, third, to_first, to_third):
+    wide = keep1.shape[1]
+    to_first[...] = keep1[...] + third[:, wide:]
+    to_third[...] = keep3[...] + first[:, wide:]
+
+
+def split_body(near, first, third, from_first, from_third, *outs):
     h = lax.axis_index("h")
+    cut = from_third.shape[0]
     inner = outs[0].shape[1]
     for t in range(SIDE):
         at = pl.ds(pl.multiple_of((h ^ t) * inner, inner), inner)
-        outs[t][...] = four([r.at[:, at] for r in (near, far0, far1, far2)])
+        outs[t][:cut] = near[:cut, at] + first[:, at] + from_third[:, at]
+        outs[t][cut:] = near[cut:, at] + third[:, at] + from_first[:, at]
 
 
 def final_body(*refs):
@@ -214,7 +228,6 @@
 
 
 VMEM = pl.BlockSpec(memory_space=pltpu.VMEM)
-HBM = pl.BlockSpec(memory_space=pltpu.HBM)
 
 
 def call(body, outs, *args, scratch=(), limit=2, name=None, flops=0, specs=None):
@@ -253,21 +266,16 @@
         v = call(swap_add_body, [(parts, *rows)], v, swap(v, "core", 1), name="sum_core")
         return lax.all_to_all(v, ("zl", "y"), 0, 0)
 
-    z_other = swap(embeddings.astype(F32), "core", 1)
+    z_own = embeddings.astype(F32)
+    z_other = swap(z_own, "core", 1)
     kern_scratch = [pltpu.VMEM((half, width), BF16), pltpu.VMEM((half, LANES), F32)]
     kern_own, row, ct, norms = call(
         own_body,
         [(half, count), (1, half), jax.ShapeDtypeStruct((width, count), BF16), (1, count)],
-        embeddings,
+        z_own,
         centres,
-        scratch=kern_scratch
-        + [
-            pltpu.VMEM((SIDE * SIDE, inner, width), BF16),
-            pltpu.VMEM((half, width), BF16),
-            pltpu.SemaphoreType.DMA((SIDE * SIDE + 1,)),
-        ],
+        scratch=kern_scratch,
         limit=16,
-        specs=[HBM, HBM],
         name="kern_own",
     )
     kern_other, row = call(
@@ -309,9 +317,11 @@
     ]
     sums = (CORES, half, 2 * LANES)
     piece = (width, SIDE * inner)
-    *far, tinv, acc = call(
+    half_piece = (width // 2, SIDE * inner)
+    pair = (width // 2, 2 * SIDE * inner)
+    first, third, keep1, keep3, tinv = call(
         far_body,
-        [piece] * 3 + [rows, sums],
+        [pair, pair, half_piece, half_piece, rows],
         kern_own,
         kern_other,
         rinv,
@@ -324,7 +334,7 @@
         limit=24,
         name="grad_far",
     )
-    far = [swap(v, "x", s) for v, s in zip(far, (1, 3, 2))]
+    first, third = swap(first, "x", 1), swap(third, "x", 3)
     near, mine, other = call(
         near_body,
         [piece, (half, width), (half, width)],
@@ -333,7 +343,6 @@
         rinv,
         finv,
         tinv,
-        acc,
         embeddings,
         z_other,
         centres,
@@ -343,18 +352,23 @@
     )
     embed = call(add_body, [mine.shape], mine, swap(other, "core", 1), name="embed_core")
     embed = call(add_body, [mine.shape], embed, swap(embed, "zl", 1), name="embed_zl")
+    to_first, to_third = call(
+        second_body, [half_piece] * 2, keep1, keep3, first, third, name="second", flops=HINT
+    )
     by_h = call(
         split_body,
         [(width, inner)] * SIDE,
         near,
-        *far,
-        embed,
-        specs=[VMEM] * SIDE + [pl.BlockSpec(memory_space=pl.ANY)],
+        first,
+        third,
+        swap(to_first, "x", 1),
+        swap(to_third, "x", 3),
         name="split",
+        flops=HINT,
     )
     embed = call(add_body, [mine.shape], embed, swap(embed, "y", 1), name="embed_y")
     embed = call(add_body, [mine.shape], embed, swap(embed, "y", 3), name="embed")
-    grad = call(final_body, [(inner, width)], *around(by_h, "h"), name="final")
+    grad = call(final_body, [(inner, width)], *around(by_h, "h"), name="final", flops=HINT)
     return embed, grad.reshape(1, inner, width)
 
 

time: 112 us -> 97.8 us (0.87)
  waiting for transfers between devices: 41.8 us -> 27.1 us
    ppermute x19 -> x20, waiting for transfers between devices: 41.8 us -> 27.1 us  [swap(): lax.ppermute(v, axis, [(i, i ^ s) for i in range(lax.axis_size(axis))])]
    ppermute x19 -> x20, starting transfers between devices: 27.3 us -> 28.2 us  [swap(): lax.ppermute(v, axis, [(i, i ^ s) for i in range(lax.axis_size(axis))])]
    unnamed x10 -> x8, local copies, waits for them, and re-layouts: 2.5 us -> 1.6 us
    pallas_call x15 -> x16, Pallas kernels: 19.4 us -> 19.8 us  [call(): pl.pallas_call(body, out_shape=shapes, in_specs=specs or [VMEM] * len(arg...]
  transfers between devices with their start and end apart: 19 -> 20, of which waited for: 14 -> 15; matrix products, arithmetic and copies ran while one was open for 0% -> 0% of each run, Pallas kernels for 5% -> 9%
where the time goes in v4:
time: 97.8 us; the launch traced here: 97.6 us
  starting transfers between devices  28.2 us (29%)
  waiting for transfers between devices  27.1 us (28%)
  Pallas kernels  19.8 us (20%)
  blocking collectives  19.2 us (20%)
  local copies, waits for them, and re-layouts  1.6 us (2%)
    ppermute x20, starting transfers between devices, swap(): lax.ppermute(v, axis, [(i, i ^ s) for i in range(lax.axis_size(axis))])  28.2 us
    ppermute x20, waiting for transfers between devices, swap(): lax.ppermute(v, axis, [(i, i ^ s) for i in range(lax.axis_size(axis))])  27.1 us
    pallas_call x16, Pallas kernels, call(): pl.pallas_call(body, out_shape=shapes, in_specs=specs or [VMEM] * len(arg...  19.8 us
    all_to_all x2, blocking collectives, over_ctr(): return lax.all_to_all(v, ('zl', 'y'), 0, 0)  19.2 us
  transfers between devices with their start and end apart: 20, of which 15 were waited for; matrix products, arithmetic and copies ran while one was open for 0% of the time, Pallas kernels for 9%

profile of v4, /device:TPU:32, one launch (start us, length us, event | category | flops | bytes accessed | tf_op | source)
XLA Modules:
  0.0 97.6 jit_solution(7067469092181247982)
XLA Ops:
  1.7 1.6 %copy-done = bf16[8192,128]{1,0:T(8,128)(2,1)S(1)} copy-done((bf16[8192,128]{1,0:T(8,128)(2,1)S(1)}, bf16[8192,128]{1,0:T(8,128)(2,1)}, u32[]{:S(2)}) %copy-start) | copy-done | bytes 2097176
  3.3 2.2 %kern_own.1 = (f32[512,4096]{1,0:T(8,128)S(1)}, f32[1,512]{1,0:T(1,128)S(1)}, bf16[128,4096]{1,0:T(8,128)(2,1)S(1)}, f32[1,4096]{1,0:T(1,128)S(1)}) custom-call(f32[512,128]{1,0:T(8,128)S(1)} %convert_element_type.3.z_ref, bf16[8192,128]{1,0:T(8,128)(2,1)S(1)} %copy-done), custom_call_target="tpu_custom_call" | custom-call | bytes 2359296 | tf_op jit(solution)/shard_map/kern_own/pallas_call | solution.py:236
  5.5 1.7 %kern_other.1 = (f32[512,4096]{1,0:T(8,128)S(1)}, f32[2,512]{1,0:T(2,128)S(1)}) custom-call(f32[512,128]{1,0:T(8,128)S(1)} %collective-permute-done.zo_ref, bf16[128,4096]{1,0:T(8,128)(2,1)S(1)} %get-tuple-element.27.ct_ref, f32[1,4096]{1,0:T(1,128)S(1)} %get-tuple-element.28.norm_ref, f32[1,512]{1,0:T(1,128)S(1)} %get-tuple-element.29.row_ref), custom_call_target="tpu_custom_call" | custom-call | bytes 1329152 | tf_op jit(solution)/shard_map/kern_other/pallas_call | solution.py:236
  8.6 10.6 %all_to_all.10.rows_ref = f32[8,2,512]{2,1,0:T(2,128)S(1)} all-to-all(f32[8,2,512]{2,1,0:T(2,128)S(1)} %sum_core.2), channel_id=1, replica_groups=mesh['x'=4,'h'=4,'core'=2,'zl'=2,'y'=4] {'zl','y'}, dimensions={0} | all-to-all | bytes 65536 | tf_op jit(solution)/shard_map/all_to_all | solution.py:267
  19.1 1.7 %freq.1 = (f32[1,4096]{1,0:T(1,128)S(1)}, f32[2,512]{1,0:T(2,128)S(1)}) custom-call(f32[512,4096]{1,0:T(8,128)S(1)} %get-tuple-element.26.own_ref, f32[512,4096]{1,0:T(8,128)S(1)} %get-tuple-element.30.other_ref, f32[8,2,512]{2,1,0:T(2,128)S(1)} %all_to_all.10.rows_ref), custom_call_target="tpu_custom_call" | custom-call | bytes 16809984 | tf_op jit(solution)/shard_map/freq/pallas_call | solution.py:236
  20.8 3.1 %collective-permute-start.4 = (f32[1,4096]{1,0:T(1,128)S(1)}, f32[1,4096]{1,0:T(1,128)S(1)}, u32[]{:S(2)}, u32[]{:S(2)}) collective-permute-start(f32[1,4096]{1,0:T(1,128)S(1)} %get-tuple-element.33.refs_0_), channel_id=1, source_target_pairs={{0,128},{64,192},{128,0},{192,64},{1,129},{65,193},{129,1},{193,65... | collective-permute-start | bytes 49160 | tf_op jit(solution)/shard_map/ppermute | solution.py:250
  26.1 2.7 %collective-permute-done.3.refs_2_ = f32[1,4096]{1,0:T(1,128)S(1)} collective-permute-done((f32[1,4096]{1,0:T(1,128)S(1)}, f32[1,4096]{1,0:T(1,128)S(1)}, u32[]{:S(2)}, u32[]{:S(2)}) %collective-permute-start.3) | collective-permute-done | bytes 16416 | tf_op jit(solution)/shard_map/ppermute | solution.py:250
  28.9 6.4 %collective-permute-start.7 = (f32[1,4096]{1,0:T(1,128)S(1)}, f32[1,4096]{1,0:T(1,128)S(1)}, u32[]{:S(2)}, u32[]{:S(2)}) collective-permute-start(f32[1,4096]{1,0:T(1,128)S(1)} %sum_x.1.f0), channel_id=1, source_target_pairs={{0,32},{16,48},{32,0},{48,16},{1,33},{17,49},{33,1},{49,17},{2,34}... | collective-permute-start | bytes 49160 | tf_op jit(solution)/shard_map/ppermute | solution.py:250
  37.0 4.1 %collective-permute-done.6.f2 = f32[1,4096]{1,0:T(1,128)S(1)} collective-permute-done((f32[1,4096]{1,0:T(1,128)S(1)}, f32[1,4096]{1,0:T(1,128)S(1)}, u32[]{:S(2)}, u32[]{:S(2)}) %collective-permute-start.6) | collective-permute-done | bytes 16416 | tf_op jit(solution)/shard_map/ppermute | solution.py:250
  41.1 1.9 %target.1 = (f32[2,512]{1,0:T(2,128)S(1)}, f32[1,4096]{1,0:T(1,128)S(1)}) custom-call(f32[512,4096]{1,0:T(8,128)S(1)} %get-tuple-element.26.own_ref, f32[512,4096]{1,0:T(8,128)S(1)} %get-tuple-element.30.other_ref, f32[1,4096]{1,0:T(1,128)S(1)} %sum_x.1.f0, f32[1,4096]{1,0:T(1,128)S(1)} %collective-permute-done.5.f1, ...), custom_call_target="tpu_custom_call" | custom-call | bytes 16875520 | tf_op jit(solution)/shard_map/target/pallas_call | solution.py:236
  44.5 8.6 %all_to_all.11.rows_ref = f32[8,2,512]{2,1,0:T(2,128)S(1)} all-to-all(f32[8,2,512]{2,1,0:T(2,128)S(1)} %sum_core.3), channel_id=1, replica_groups=mesh['x'=4,'h'=4,'core'=2,'zl'=2,'y'=4] {'zl','y'}, dimensions={0} | all-to-all | bytes 65536 | tf_op jit(solution)/shard_map/all_to_all | solution.py:267
  53.1 4.6 %grad_far.1 = (f32[64,2048]{1,0:T(8,128)S(1)}, f32[64,2048]{1,0:T(8,128)S(1)}, f32[64,1024]{1,0:T(8,128)S(1)}, f32[64,1024]{1,0:T(8,128)S(1)}, f32[2,512]{1,0:T(2,128)S(1)}) custom-call(f32[512,4096]{1,0:T(8,128)S(1)} %get-tuple-element.26.own_ref, f32[512,4096]{1,0:T(8,128)S(1)} %get-tuple-element.30.other_ref, f32[2,512]{1,0:T(2,128)S(1)} %get-tuple-element.32.rinv_ref, ...), custom_call_target="tpu_custom_call" | custom-call | bytes 19320832 | tf_op jit(solution)/shard_map/grad_far/pallas_call | solution.py:236
  57.8 2.1 %collective-permute-start.14 = (f32[64,2048]{1,0:T(8,128)S(1)}, f32[64,2048]{1,0:T(8,128)S(1)}, u32[]{:S(2)}, u32[]{:S(2)}) collective-permute-start(f32[64,2048]{1,0:T(8,128)S(1)} %get-tuple-element.41), channel_id=1, source_target_pairs={{0,192},{64,128},{128,64},{192,0},{1,193},{65,129},{129,65},{193,1... | collective-permute-start | bytes 1572872 | tf_op jit(solution)/shard_map/ppermute | solution.py:250
  59.9 6.0 %grad_near.1 = (f32[128,1024]{1,0:T(8,128)S(1)}, f32[512,128]{1,0:T(8,128)S(1)}, f32[512,128]{1,0:T(8,128)S(1)}) custom-call(f32[512,4096]{1,0:T(8,128)S(1)} %get-tuple-element.26.own_ref, f32[512,4096]{1,0:T(8,128)S(1)} %get-tuple-element.30.other_ref, f32[2,512]{1,0:T(2,128)S(1)} %get-tuple-element.32.rinv_ref, f32[1,4096]{1,0:T(1,128)S(1)} %get-tuple-element.34.finv_ref, ...), custom_call_target="tpu_custom_call" | custom-call | bytes 19292160 | tf_op jit(solution)/shard_map/grad_near/pallas_call | solution.py:236
  66.0 1.5 %collective-permute-done.9.refs_1_ = f32[512,128]{1,0:T(8,128)S(1)} collective-permute-done((f32[512,128]{1,0:T(8,128)S(1)}, f32[512,128]{1,0:T(8,128)S(1)}, u32[]{:S(2)}, u32[]{:S(2)}) %collective-permute-start.9) | collective-permute-done | bytes 262176 | tf_op jit(solution)/shard_map/ppermute | solution.py:250
  67.6 1.7 %collective-permute-start.10 = (f32[512,128]{1,0:T(8,128)S(1)}, f32[512,128]{1,0:T(8,128)S(1)}, u32[]{:S(2)}, u32[]{:S(2)}) collective-permute-start(f32[512,128]{1,0:T(8,128)S(1)} %embed_core.1.refs_0_), channel_id=1, source_target_pairs={{0,4},{4,0},{1,5},{5,1},{2,6},{6,2},{3,7},{7,3},{8,12},{12,8},{9,1... | collective-permute-start | bytes 786440 | tf_op jit(solution)/shard_map/ppermute | solution.py:250
  72.5 2.0 %collective-permute-start.16 = (f32[64,1024]{1,0:T(8,128)S(1)}, f32[64,1024]{1,0:T(8,128)S(1)}, u32[]{:S(2)}, u32[]{:S(2)}) collective-permute-start(f32[64,1024]{1,0:T(8,128)S(1)} %get-tuple-element.45), channel_id=1, source_target_pairs={{0,192},{64,128},{128,64},{192,0},{1,193},{65,129},{129,65},{193,1... | collective-permute-start | bytes 786440 | tf_op jit(solution)/shard_map/ppermute | solution.py:250
  74.6 1.6 %collective-permute-done.10.refs_1_ = f32[512,128]{1,0:T(8,128)S(1)} collective-permute-done((f32[512,128]{1,0:T(8,128)S(1)}, f32[512,128]{1,0:T(8,128)S(1)}, u32[]{:S(2)}, u32[]{:S(2)}) %collective-permute-start.10) | collective-permute-done | bytes 262176 | tf_op jit(solution)/shard_map/ppermute | solution.py:250
  76.9 1.5 %collective-permute-done.15.from_first = f32[64,1024]{1,0:T(8,128)S(1)} collective-permute-done((f32[64,1024]{1,0:T(8,128)S(1)}, f32[64,1024]{1,0:T(8,128)S(1)}, u32[]{:S(2)}, u32[]{:S(2)}) %collective-permute-start.15) | collective-permute-done | bytes 262176 | tf_op jit(solution)/shard_map/ppermute | solution.py:250
  78.5 1.6 %collective-permute-done.16.from_third = f32[64,1024]{1,0:T(8,128)S(1)} collective-permute-done((f32[64,1024]{1,0:T(8,128)S(1)}, f32[64,1024]{1,0:T(8,128)S(1)}, u32[]{:S(2)}, u32[]{:S(2)}) %collective-permute-start.16) | collective-permute-done | bytes 262176 | tf_op jit(solution)/shard_map/ppermute | solution.py:250
  80.2 1.7 %collective-permute-start.17 = (f32[128,256]{1,0:T(8,128)S(1)}, f32[128,256]{1,0:T(8,128)S(1)}, u32[]{:S(2)}, u32[]{:S(2)}) collective-permute-start(f32[128,256]{1,0:T(8,128)S(1)} %get-tuple-element.47), channel_id=1, source_target_pairs={{0,16},{16,0},{32,48},{48,32},{1,17},{17,1},{33,49},{49,33},{2,18}... | collective-permute-start | bytes 393224 | tf_op jit(solution)/shard_map/ppermute | solution.py:250
  82.0 2.9 %collective-permute-start.18 = (f32[128,256]{1,0:T(8,128)S(1)}, f32[128,256]{1,0:T(8,128)S(1)}, u32[]{:S(2)}, u32[]{:S(2)}) collective-permute-start(f32[128,256]{1,0:T(8,128)S(1)} %get-tuple-element.48), channel_id=1, source_target_pairs={{0,48},{16,32},{32,16},{48,0},{1,49},{17,33},{33,17},{49,1},{2,50}... | collective-permute-start | bytes 393224 | tf_op jit(solution)/shard_map/ppermute | solution.py:250
  84.9 1.9 %collective-permute-start.19 = (f32[128,256]{1,0:T(8,128)S(1)}, f32[128,256]{1,0:T(8,128)S(1)}, u32[]{:S(2)}, u32[]{:S(2)}) collective-permute-start(f32[128,256]{1,0:T(8,128)S(1)} %get-tuple-element.49), channel_id=1, source_target_pairs={{0,32},{16,48},{32,0},{48,16},{1,33},{17,49},{33,1},{49,17},{2,34}... | collective-permute-start | bytes 393224 | tf_op jit(solution)/shard_map/ppermute | solution.py:250
  89.6 6.5 %collective-permute-done.18.refs_2_ = f32[128,256]{1,0:T(8,128)S(1)} collective-permute-done((f32[128,256]{1,0:T(8,128)S(1)}, f32[128,256]{1,0:T(8,128)S(1)}, u32[]{:S(2)}, u32[]{:S(2)}) %collective-permute-start.18) | collective-permute-done | bytes 131104 | tf_op jit(solution)/shard_map/ppermute | solution.py:250
  (43 shorter events, 16.4 us)
Async XLA Ops:
  1.6 3.9 %collective-permute-start = (f32[512,128]{1,0:T(8,128)S(1)}, f32[512,128]{1,0:T(8,128)S(1)}, u32[]{:S(2)}, u32[]{:S(2)}) collective-permute-start(f32[512,128]{1,0:T(8,128)S(1)} %convert_element_type.3.z_ref), channel_id=1, source_target_pairs={{0,8},{8,0},{1,9},{9,1},{2,10},{10,2},{3,11},{11,3},{4,12},{12,4},... | collective-permute-start | bytes 786440 | tf_op jit(solution)/shard_map/ppermute | solution.py:250
  1.7 1.6 %copy-start = (bf16[8192,128]{1,0:T(8,128)(2,1)S(1)}, bf16[8192,128]{1,0:T(8,128)(2,1)}, u32[]{:S(2)}) copy-start(bf16[8192,128]{1,0:T(8,128)(2,1)} %c_ref.5) | copy-start | bytes 6291460
  7.1 1.4 %collective-permute-start.1 = (f32[2,512]{1,0:T(2,128)S(1)}, f32[2,512]{1,0:T(2,128)S(1)}, u32[]{:S(2)}, u32[]{:S(2)}) collective-permute-start(f32[2,512]{1,0:T(2,128)S(1)} %get-tuple-element.31.mine), channel_id=1, source_target_pairs={{0,8},{8,0},{1,9},{9,1},{2,10},{10,2},{3,11},{11,3},{4,12},{12,4},... | collective-permute-start | bytes 12296 | tf_op jit(solution)/shard_map/ppermute | solution.py:250
  19.1 22.0 %copy-start.3 = (f32[8192]{0:T(1024)S(1)}, f32[8192]{0:T(1024)}, u32[]{:S(2)}) copy-start(f32[8192]{0:T(1024)} %param.5) | copy-start | bytes 98308
  20.8 5.3 %collective-permute-start.4 = (f32[1,4096]{1,0:T(1,128)S(1)}, f32[1,4096]{1,0:T(1,128)S(1)}, u32[]{:S(2)}, u32[]{:S(2)}) collective-permute-start(f32[1,4096]{1,0:T(1,128)S(1)} %get-tuple-element.33.refs_0_), channel_id=1, source_target_pairs={{0,128},{64,192},{128,0},{192,64},{1,129},{65,193},{129,1},{193,65... | collective-permute-start | bytes 49160 | tf_op jit(solution)/shard_map/ppermute | solution.py:250
  23.9 4.9 %collective-permute-start.3 = (f32[1,4096]{1,0:T(1,128)S(1)}, f32[1,4096]{1,0:T(1,128)S(1)}, u32[]{:S(2)}, u32[]{:S(2)}) collective-permute-start(f32[1,4096]{1,0:T(1,128)S(1)} %get-tuple-element.33.refs_0_), channel_id=1, source_target_pairs={{0,192},{64,128},{128,64},{192,0},{1,193},{65,129},{129,65},{193,1... | collective-permute-start | bytes 49160 | tf_op jit(solution)/shard_map/ppermute | solution.py:250
  25.1 3.8 %collective-permute-start.2 = (f32[1,4096]{1,0:T(1,128)S(1)}, f32[1,4096]{1,0:T(1,128)S(1)}, u32[]{:S(2)}, u32[]{:S(2)}) collective-permute-start(f32[1,4096]{1,0:T(1,128)S(1)} %get-tuple-element.33.refs_0_), channel_id=1, source_target_pairs={{0,64},{64,0},{128,192},{192,128},{1,65},{65,1},{129,193},{193,129... | collective-permute-start | bytes 49160 | tf_op jit(solution)/shard_map/ppermute | solution.py:250
  28.9 8.1 %collective-permute-start.7 = (f32[1,4096]{1,0:T(1,128)S(1)}, f32[1,4096]{1,0:T(1,128)S(1)}, u32[]{:S(2)}, u32[]{:S(2)}) collective-permute-start(f32[1,4096]{1,0:T(1,128)S(1)} %sum_x.1.f0), channel_id=1, source_target_pairs={{0,32},{16,48},{32,0},{48,16},{1,33},{17,49},{33,1},{49,17},{2,34}... | collective-permute-start | bytes 49160 | tf_op jit(solution)/shard_map/ppermute | solution.py:250
  35.2 5.8 %collective-permute-start.6 = (f32[1,4096]{1,0:T(1,128)S(1)}, f32[1,4096]{1,0:T(1,128)S(1)}, u32[]{:S(2)}, u32[]{:S(2)}) collective-permute-start(f32[1,4096]{1,0:T(1,128)S(1)} %sum_x.1.f0), channel_id=1, source_target_pairs={{0,48},{16,32},{32,16},{48,0},{1,49},{17,33},{33,17},{49,1},{2,50}... | collective-permute-start | bytes 49160 | tf_op jit(solution)/shard_map/ppermute | solution.py:250
  35.8 5.3 %collective-permute-start.5 = (f32[1,4096]{1,0:T(1,128)S(1)}, f32[1,4096]{1,0:T(1,128)S(1)}, u32[]{:S(2)}, u32[]{:S(2)}) collective-permute-start(f32[1,4096]{1,0:T(1,128)S(1)} %sum_x.1.f0), channel_id=1, source_target_pairs={{0,16},{16,0},{32,48},{48,32},{1,17},{17,1},{33,49},{49,33},{2,18}... | collective-permute-start | bytes 49160 | tf_op jit(solution)/shard_map/ppermute | solution.py:250
  41.1 12.0 %copy-start.1 = (bf16[8192,128]{1,0:T(8,128)(2,1)S(1)}, bf16[8192,128]{1,0:T(8,128)(2,1)}, u32[]{:S(2)}) copy-start(bf16[8192,128]{1,0:T(8,128)(2,1)} %c_ref.5) | copy-start | bytes 6291460
  41.1 12.0 %copy-start.2 = (bf16[512,128]{1,0:T(8,128)(2,1)S(1)}, bf16[512,128]{1,0:T(8,128)(2,1)}, u32[]{:S(2)}) copy-start(bf16[512,128]{1,0:T(8,128)(2,1)} %z_ref.3) | copy-start | bytes 393220
  43.0 1.4 %collective-permute-start.8 = (f32[2,512]{1,0:T(2,128)S(1)}, f32[2,512]{1,0:T(2,128)S(1)}, u32[]{:S(2)}, u32[]{:S(2)}) collective-permute-start(f32[2,512]{1,0:T(2,128)S(1)} %get-tuple-element.35.mine), channel_id=1, source_target_pairs={{0,8},{8,0},{1,9},{9,1},{2,10},{10,2},{3,11},{11,3},{4,12},{12,4},... | collective-permute-start | bytes 12296 | tf_op jit(solution)/shard_map/ppermute | solution.py:250
  57.7 12.9 %collective-permute-start.13 = (f32[64,2048]{1,0:T(8,128)S(1)}, f32[64,2048]{1,0:T(8,128)S(1)}, u32[]{:S(2)}, u32[]{:S(2)}) collective-permute-start(f32[64,2048]{1,0:T(8,128)S(1)} %get-tuple-element.40), channel_id=1, source_target_pairs={{0,64},{64,0},{128,192},{192,128},{1,65},{65,1},{129,193},{193,129... | collective-permute-start | bytes 1572872 | tf_op jit(solution)/shard_map/ppermute | solution.py:250
  57.8 14.1 %collective-permute-start.14 = (f32[64,2048]{1,0:T(8,128)S(1)}, f32[64,2048]{1,0:T(8,128)S(1)}, u32[]{:S(2)}, u32[]{:S(2)}) collective-permute-start(f32[64,2048]{1,0:T(8,128)S(1)} %get-tuple-element.41), channel_id=1, source_target_pairs={{0,192},{64,128},{128,64},{192,0},{1,193},{65,129},{129,65},{193,1... | collective-permute-start | bytes 1572872 | tf_op jit(solution)/shard_map/ppermute | solution.py:250
  65.9 1.6 %collective-permute-start.9 = (f32[512,128]{1,0:T(8,128)S(1)}, f32[512,128]{1,0:T(8,128)S(1)}, u32[]{:S(2)}, u32[]{:S(2)}) collective-permute-start(f32[512,128]{1,0:T(8,128)S(1)} %get-tuple-element.38), channel_id=1, source_target_pairs={{0,8},{8,0},{1,9},{9,1},{2,10},{10,2},{3,11},{11,3},{4,12},{12,4},... | collective-permute-start | bytes 786440 | tf_op jit(solution)/shard_map/ppermute | solution.py:250
  67.6 8.7 %collective-permute-start.10 = (f32[512,128]{1,0:T(8,128)S(1)}, f32[512,128]{1,0:T(8,128)S(1)}, u32[]{:S(2)}, u32[]{:S(2)}) collective-permute-start(f32[512,128]{1,0:T(8,128)S(1)} %embed_core.1.refs_0_), channel_id=1, source_target_pairs={{0,4},{4,0},{1,5},{5,1},{2,6},{6,2},{3,7},{7,3},{8,12},{12,8},{9,1... | collective-permute-start | bytes 786440 | tf_op jit(solution)/shard_map/ppermute | solution.py:250
  72.0 6.5 %collective-permute-start.15 = (f32[64,1024]{1,0:T(8,128)S(1)}, f32[64,1024]{1,0:T(8,128)S(1)}, u32[]{:S(2)}, u32[]{:S(2)}) collective-permute-start(f32[64,1024]{1,0:T(8,128)S(1)} %get-tuple-element.44), channel_id=1, source_target_pairs={{0,64},{64,0},{128,192},{192,128},{1,65},{65,1},{129,193},{193,129... | collective-permute-start | bytes 786440 | tf_op jit(solution)/shard_map/ppermute | solution.py:250
  72.5 7.6 %collective-permute-start.16 = (f32[64,1024]{1,0:T(8,128)S(1)}, f32[64,1024]{1,0:T(8,128)S(1)}, u32[]{:S(2)}, u32[]{:S(2)}) collective-permute-start(f32[64,1024]{1,0:T(8,128)S(1)} %get-tuple-element.45), channel_id=1, source_target_pairs={{0,192},{64,128},{128,64},{192,0},{1,193},{65,129},{129,65},{193,1... | collective-permute-start | bytes 786440 | tf_op jit(solution)/shard_map/ppermute | solution.py:250
  76.3 10.6 %collective-permute-start.11 = (f32[512,128]{1,0:T(8,128)S(1)}, f32[512,128]{1,0:T(8,128)S(1)}, u32[]{:S(2)}, u32[]{:S(2)}) collective-permute-start(f32[512,128]{1,0:T(8,128)S(1)} %embed_zl.1.refs_0_), channel_id=1, source_target_pairs={{0,1},{1,0},{2,3},{3,2},{4,5},{5,4},{6,7},{7,6},{8,9},{9,8},{10,11... | collective-permute-start | bytes 786440 | tf_op jit(solution)/shard_map/ppermute | solution.py:250
  80.2 9.3 %collective-permute-start.17 = (f32[128,256]{1,0:T(8,128)S(1)}, f32[128,256]{1,0:T(8,128)S(1)}, u32[]{:S(2)}, u32[]{:S(2)}) collective-permute-start(f32[128,256]{1,0:T(8,128)S(1)} %get-tuple-element.47), channel_id=1, source_target_pairs={{0,16},{16,0},{32,48},{48,32},{1,17},{17,1},{33,49},{49,33},{2,18}... | collective-permute-start | bytes 393224 | tf_op jit(solution)/shard_map/ppermute | solution.py:250
  82.0 14.1 %collective-permute-start.18 = (f32[128,256]{1,0:T(8,128)S(1)}, f32[128,256]{1,0:T(8,128)S(1)}, u32[]{:S(2)}, u32[]{:S(2)}) collective-permute-start(f32[128,256]{1,0:T(8,128)S(1)} %get-tuple-element.48), channel_id=1, source_target_pairs={{0,48},{16,32},{32,16},{48,0},{1,49},{17,33},{33,17},{49,1},{2,50}... | collective-permute-start | bytes 393224 | tf_op jit(solution)/shard_map/ppermute | solution.py:250
  84.9 11.2 %collective-permute-start.19 = (f32[128,256]{1,0:T(8,128)S(1)}, f32[128,256]{1,0:T(8,128)S(1)}, u32[]{:S(2)}, u32[]{:S(2)}) collective-permute-start(f32[128,256]{1,0:T(8,128)S(1)} %get-tuple-element.49), channel_id=1, source_target_pairs={{0,32},{16,48},{32,0},{48,16},{1,33},{17,49},{33,1},{49,17},{2,34}... | collective-permute-start | bytes 393224 | tf_op jit(solution)/shard_map/ppermute | solution.py:250
  86.9 10.0 %collective-permute-start.12 = (f32[512,128]{1,0:T(8,128)S(1)}, f32[512,128]{1,0:T(8,128)S(1)}, u32[]{:S(2)}, u32[]{:S(2)}) collective-permute-start(f32[512,128]{1,0:T(8,128)S(1)} %embed_y.1.refs_0_), channel_id=1, source_target_pairs={{0,3},{1,2},{2,1},{3,0},{4,7},{5,6},{6,5},{7,4},{8,11},{9,10},{10,... | collective-permute-start | bytes 786440 | tf_op jit(solution)/shard_map/ppermute | solution.py:250
